TPU v7x, 32 devices: a whole 2x2x4 slice. The times are simulated.
32 devices in a mesh: groups: 2 (over y), tiles: 8 (over z, x), subwin: 2 (over core).
Axes of the slice: x: 2, y: 2, z: 4, core: 2. Of those that a mesh axis runs over, the one named last changes fastest.
Arguments:
- increment: float32 [64, 8, 16, 16], P(('groups', 'tiles'), 'subwin'), parts along dimension 0, may hold values from -6 to 6
- dual_vector: float32 [64, 8, 16, 16], P(('groups', 'tiles'), 'subwin'), parts along dimension 0, may hold values from -6 to 6
- wind_u: float32 [32, 16, 16], P('tiles'), may hold values from -0.3 to 0.3
- wind_v: float32 [32, 16, 16], P('tiles'), may hold values from -0.3 to 0.3
- land_sea: int32 [32, 16], P('tiles'), may hold values from 0 to 1
- length_sq: float32 [8, 16], P('subwin', 'tiles'), may hold values from 1 to 300
- spread: float32 [8, 16], P('subwin'), may hold values from 0.5 to 3
Outputs:
- model_side: float32 [64, 8, 16, 16], P(('groups', 'tiles'), 'subwin'), parts along dimension 0
- dual_side: float32 [64, 8, 16, 16], P(('groups', 'tiles'), 'subwin'), parts along dimension 0
There are 2 independent parts, one for each index of `groups`. A program takes and returns all parts, laid end to end along the dimension named above; an argument that names none is the same for every part. Nothing has to cross between parts.
All inputs are finite; a program needn't handle non-finite values.
Results may differ from a plain program's by a relative error of at most 0.000098.
Values sent between devices are 32-bit elements; how exact they have to be, the bound alone decides.
A program may use at most 192 MiB of HBM per device.

v0:
```python
import math

import jax
import jax.numpy as jnp
from jax import lax
from jax.sharding import PartitionSpec as P

STEPS = 8
SWEEPS = 4
LON_DEV = 4


def extended(x, sides, width):
    for axis, dim in sides:
        devices, length = (lax.axis_size(axis), x.shape[dim])
        up = [(i, (i + 1) % devices) for i in range(devices)]
        down = [(j, i) for i, j in up]
        last = lax.slice_in_dim(x, length - width, length, axis=dim)
        leading = lax.slice_in_dim(x, 0, width, axis=dim)
        before = lax.ppermute(last, axis, up)
        after = lax.ppermute(leading, axis, down)
        x = jnp.concatenate([before, x, after], axis=dim)
    return x


def passed_along(x, axis, by):
    devices = lax.axis_size(axis)
    pairs = [(i, i + by) for i in range(devices) if 0 <= i + by < devices]
    return lax.ppermute(x, axis, pairs)


def from_north(values):
    return jnp.concatenate([values[..., 1:], jnp.zeros_like(values[..., :1])], axis=-1)


def from_south(values):
    return jnp.concatenate([jnp.zeros_like(values[..., :1]), values[..., :-1]], axis=-1)


def coefficients(wind_u, wind_v, mixing):
    return (
        1.0 - 4.0 * mixing,
        mixing - 0.5 * wind_u,
        mixing + 0.5 * wind_u,
        mixing - 0.5 * wind_v,
        mixing + 0.5 * wind_v,
    )


def tangent_step(fields, coeffs, offset):
    extent = fields.shape[0]
    centre, eastward, westward, northward, southward = [
        coeff[offset + 1 : offset + extent - 1][:, None] for coeff in coeffs
    ]
    middle = fields[1:-1]
    return (
        centre * middle
        + eastward * fields[2:]
        + westward * fields[:-2]
        + northward * from_north(middle)
        + southward * from_south(middle)
    )


def adjoint_step(fields, coeffs, offset):
    extent = fields.shape[0]
    centre = coeffs[0][offset + 1 : offset + extent - 1][:, None]
    northward = coeffs[3][offset + 1 : offset + extent - 1][:, None]
    southward = coeffs[4][offset + 1 : offset + extent - 1][:, None]
    eastward = coeffs[1][offset : offset + extent][:, None]
    westward = coeffs[2][offset : offset + extent][:, None]
    middle = fields[1:-1]
    return (
        centre * middle
        + (eastward * fields)[:-2]
        + (westward * fields)[2:]
        + from_south(northward * middle)
        + from_north(southward * middle)
    )


def run_tangent(fields, coeffs, margin):
    for repeat in range(STEPS // margin):
        grown = extended(fields, (("tiles", 0),), margin)
        for inner_step in range(margin):
            offset = (coeffs[0].shape[0] - grown.shape[0]) // 2
            grown = tangent_step(grown, coeffs, offset)
        fields = grown
    return fields


def run_adjoint(fields, coeffs, margin):
    for repeat in range(STEPS // margin):
        grown = extended(fields, (("tiles", 0),), margin)
        for inner_step in range(margin):
            offset = (coeffs[0].shape[0] - grown.shape[0]) // 2
            grown = adjoint_step(grown, coeffs, offset)
        fields = grown
    return fields


def square_tables(extent):
    index = jnp.arange(extent, dtype=jnp.int32)
    phases = index[:, None] * index[None, :] % extent
    angles = phases.astype(jnp.float32) * (2.0 * math.pi / extent)
    return (jnp.cos(angles), jnp.sin(angles))


def contract(form, first, second):
    return jnp.einsum(form, first, second, precision=lax.Precision.HIGHEST)


def smooth_bands(bands, length_sq):
    count = bands.shape[0]
    inner = LON_DEV
    outer = count // inner
    columns = bands.reshape(outer, inner, -1)
    cos_outer, sin_outer = square_tables(outer)
    cos_inner, sin_inner = square_tables(inner)
    outer_index = jnp.arange(outer, dtype=jnp.int32)
    inner_index = jnp.arange(inner, dtype=jnp.int32)
    twist = (outer_index[:, None] * inner_index[None, :] % count).astype(jnp.float32) * (
        2.0 * math.pi / count
    )
    twist_cos = jnp.cos(twist)[:, :, None]
    twist_sin = jnp.sin(twist)[:, :, None]
    first_real = contract("ab,bqc->aqc", cos_outer, columns)
    first_imag = -contract("ab,bqc->aqc", sin_outer, columns)
    turned_real = first_real * twist_cos + first_imag * twist_sin
    turned_imag = first_imag * twist_cos - first_real * twist_sin
    modes_real = contract("aqc,kq->akc", turned_real, cos_inner) + contract(
        "aqc,kq->akc", turned_imag, sin_inner
    )
    modes_imag = contract("aqc,kq->akc", turned_imag, cos_inner) - contract(
        "aqc,kq->akc", turned_real, sin_inner
    )
    wave = (outer_index[:, None] + outer * inner_index[None, :]).astype(jnp.float32)
    basic = 1.0 - jnp.cos(wave * (2.0 * math.pi / count))
    damping = (1.0 + 2.0 * length_sq[None, None, :, None, :] * basic[:, :, None, None, None]) ** (
        -SWEEPS
    )
    damping = jnp.broadcast_to(damping, (outer, inner) + bands.shape[1:]).reshape(outer, inner, -1)
    modes_real = modes_real * damping
    modes_imag = modes_imag * damping
    back_real = contract("akc,kq->aqc", modes_real, cos_inner) - contract(
        "akc,kq->aqc", modes_imag, sin_inner
    )
    back_imag = contract("akc,kq->aqc", modes_imag, cos_inner) + contract(
        "akc,kq->aqc", modes_real, sin_inner
    )
    final_real = back_real * twist_cos - back_imag * twist_sin
    final_imag = back_imag * twist_cos + back_real * twist_sin
    smoothed = contract("ab,bqc->aqc", cos_outer, final_real) - contract(
        "ab,bqc->aqc", sin_outer, final_imag
    )
    return (smoothed / count).reshape(bands.shape)


def body(increment, dual_vector, wind_u, wind_v, land_sea, length_sq, spread):
    margin = 4
    mixing = 0.15 + 0.09 * land_sea.astype(jnp.float32)
    grown_u, grown_v, grown_mix = (
        extended(wind_u, (("tiles", 0),), margin),
        extended(wind_v, (("tiles", 0),), margin),
        extended(mixing, (("tiles", 0),), margin),
    )
    coeffs = coefficients(grown_u, grown_v, grown_mix[:, None, :])
    carried = passed_along(increment[:, -1:], "subwin", 1)
    previous = jnp.concatenate([carried, increment[:, :-1]], axis=1)
    later = passed_along(dual_vector[:, :1], "subwin", -1)
    following = jnp.concatenate([dual_vector[:, 1:], later], axis=1)
    weighted = dual_vector * spread[None, :, :, None]
    bands = lax.all_to_all(weighted, "tiles", split_axis=3, concat_axis=0, tiled=True)
    smoothed = smooth_bands(bands, length_sq)
    forward = run_tangent(previous, coeffs, margin)
    backward = run_adjoint(following, coeffs, margin)
    returned = lax.all_to_all(smoothed, "tiles", split_axis=0, concat_axis=3, tiled=True)
    covar = returned * spread[None, :, :, None]
    return (covar + increment - forward, dual_vector - backward)


def solution(mesh):
    placed = (
        P(("groups", "tiles"), "subwin", None, None),
        P(("groups", "tiles"), "subwin", None, None),
        P("tiles", None, None),
        P("tiles", None, None),
        P("tiles", None),
        P("subwin", "tiles"),
        P("subwin", None),
    )
    return jax.shard_map(
        body,
        mesh=mesh,
        in_specs=placed,
        out_specs=(
            P(("groups", "tiles"), "subwin", None, None),
            P(("groups", "tiles"), "subwin", None, None),
        ),
        check_vma=False,
    )
```

profile of v0, /device:TPU:0, one launch (start us, length us, event | category | flops | bytes accessed | tf_op | source)
XLA Modules:
  0.0 88.9 jit_solution(5874913392847764511)
XLA Ops:
  0.6 0.7 fusion.186
  1.3 2.9 %collective-permute-start = (f32[4,16]{1,0:T(4,128)S(1)}, f32[4,16]{1,0:T(4,128)S(1)}, u32[]{:S(2)}, u32[]{:S(2)}) collective-permute-start(f32[4,16]{1,0:T(4,128)S(1)} %get-tuple-element.69), channel_id=1, source_target_pairs={{0,2},{2,4},{4,6},{6,8},{8,10},{10,12},{12,14},{14,0},{1,3},{3,5},... | collective-permute-start | bytes 776 | tf_op jit(solution)/shard_map/ppermute | solution.py:20
  4.3 3.0 %collective-permute-start.1 = (f32[4,16]{1,0:T(4,128)S(1)}, f32[4,16]{1,0:T(4,128)S(1)}, u32[]{:S(2)}, u32[]{:S(2)}) collective-permute-start(f32[4,16]{1,0:T(4,128)S(1)} %get-tuple-element.69), channel_id=1, source_target_pairs={{2,0},{4,2},{6,4},{8,6},{10,8},{12,10},{14,12},{0,14},{3,1},{5,3},... | collective-permute-start | bytes 776 | tf_op jit(solution)/shard_map/ppermute | solution.py:21
  7.3 4.7 %collective-permute-start.6 = (f32[4,16,16]{2,1,0:T(8,128)}, f32[4,16,16]{2,1,0:T(8,128)S(1)}, u32[]{:S(2)}, u32[]{:S(2)}) collective-permute-start(f32[4,16,16]{2,1,0:T(8,128)} %param.9), channel_id=1, source_target_pairs={{2,0},{4,2},{6,4},{8,6},{10,8},{12,10},{14,12},{0,14},{3,1},{5,3},... | collective-permute-start | bytes 12296 | tf_op jit(solution)/shard_map/ppermute | solution.py:21
  12.0 1.0 %copy.123 = f32[4,4,16,16]{2,3,1,0:T(8,128)S(1)} copy(f32[4,4,16,16]{3,2,1,0:T(8,128)} %param.8) | data formatting | bytes 32768 | tf_op args[1]
  13.1 0.7 copy-done.6
  14.8 4.7 %collective-permute-start.8 = (f32[4,16,16]{2,1,0:T(8,128)S(1)}, f32[4,16,16]{2,1,0:T(8,128)S(1)}, u32[]{:S(2)}, u32[]{:S(2)}) collective-permute-start(f32[4,16,16]{2,1,0:T(8,128)S(1)} %copy-done.4), channel_id=1, source_target_pairs={{2,0},{4,2},{6,4},{8,6},{10,8},{12,10},{14,12},{0,14},{3,1},{5,3},... | collective-permute-start | bytes 12296 | tf_op jit(solution)/shard_map/ppermute | solution.py:21
  19.5 1.3 %collective-permute-start.11 = (f32[4,1,16,16]{2,3,1,0:T(8,128)S(1)}, f32[4,1,16,16]{2,3,1,0:T(8,128)S(1)}, u32[]{:S(2)}, u32[]{:S(2)}) collective-permute-start(f32[4,1,16,16]{2,3,1,0:T(8,128)S(1)} %slice.551), channel_id=1, source_target_pairs={{1,0},{3,2},{5,4},{7,6},{9,8},{11,10},{13,12},{15,14},{17,16},{19,... | collective-permute-start | bytes 12296 | tf_op jit(solution)/shard_map/ppermute | solution.py:29
  20.9 1.7 %collective-permute-done.11 = f32[4,1,16,16]{2,3,1,0:T(8,128)S(1)} collective-permute-done((f32[4,1,16,16]{2,3,1,0:T(8,128)S(1)}, f32[4,1,16,16]{2,3,1,0:T(8,128)S(1)}, u32[]{:S(2)}, u32[]{:S(2)}) %collective-permute-start.11) | collective-permute-done | bytes 4128 | tf_op jit(solution)/shard_map/ppermute | solution.py:29
  22.6 2.1 %collective-permute-start.2 = (f32[4,1,16,16]{2,3,1,0:T(8,128)S(1)}, f32[4,1,16,16]{2,3,1,0:T(8,128)S(1)}, u32[]{:S(2)}, u32[]{:S(2)}) collective-permute-start(f32[4,1,16,16]{2,3,1,0:T(8,128)S(1)} %slice.492), channel_id=1, source_target_pairs={{0,1},{2,3},{4,5},{6,7},{8,9},{10,11},{12,13},{14,15},{16,17},{18,... | collective-permute-start | bytes 12296 | tf_op jit(solution)/shard_map/ppermute | solution.py:29
  24.7 0.8 collective-permute-done.2
  25.6 4.8 %collective-permute-start.13 = (f32[4,4,16,16]{2,3,1,0:T(8,128)S(1)}, f32[4,4,16,16]{2,3,1,0:T(8,128)S(1)}, u32[]{:S(2)}, u32[]{:S(2)}) collective-permute-start(f32[4,4,16,16]{2,3,1,0:T(8,128)S(1)} %pad_maximum_fusion.5), channel_id=1, source_target_pairs={{2,0},{4,2},{6,4},{8,6},{10,8},{12,10},{14,12},{0,14},{3,1},{5,3},... | collective-permute-start | bytes 49160 | tf_op jit(solution)/shard_map/ppermute | solution.py:21
  30.3 4.7 %collective-permute-start.4 = (f32[4,4,16,16]{2,3,1,0:T(8,128)S(1)}, f32[4,4,16,16]{2,3,1,0:T(8,128)S(1)}, u32[]{:S(2)}, u32[]{:S(2)}) collective-permute-start(f32[4,4,16,16]{2,3,1,0:T(8,128)S(1)} %pad_maximum_fusion.4), channel_id=1, source_target_pairs={{2,0},{4,2},{6,4},{8,6},{10,8},{12,10},{14,12},{0,14},{3,1},{5,3},... | collective-permute-start | bytes 49160 | tf_op jit(solution)/shard_map/ppermute | solution.py:21
  37.0 0.8 copy-done
  38.3 1.5 %collective-permute-done.4 = f32[4,4,16,16]{2,3,1,0:T(8,128)S(1)} collective-permute-done((f32[4,4,16,16]{2,3,1,0:T(8,128)S(1)}, f32[4,4,16,16]{2,3,1,0:T(8,128)S(1)}, u32[]{:S(2)}, u32[]{:S(2)}) %collective-permute-start.4) | collective-permute-done | bytes 16416 | tf_op jit(solution)/shard_map/ppermute | solution.py:21
  39.9 0.9 %slice-done = f32[10,4,16,16]{2,3,1,0:T(8,128)S(1)} async-done(((f32[12,4,16,16]{2,3,1,0:T(8,128)}), f32[10,4,16,16]{2,3,1,0:T(8,128)S(1)}, s32[]{:S(2)}) %slice-start) | async-done | bytes 40984 | tf_op jit(solution)/shard_map/slice | solution.py:72
  40.9 0.9 %copy-done.1 = f32[12,4,16,16]{2,3,1,0:T(8,128)S(1)} copy-done((f32[12,4,16,16]{2,3,1,0:T(8,128)S(1)}, f32[12,4,16,16]{2,3,1,0:T(8,128)}, u32[]{:S(2)}) %copy-start.1) | copy-done | bytes 49176
  43.5 3.0 %collective-permute-start.10 = (f32[4,4,16,16]{2,3,1,0:T(8,128)S(1)}, f32[4,4,16,16]{2,3,1,0:T(8,128)S(1)}, u32[]{:S(2)}, u32[]{:S(2)}) collective-permute-start(f32[4,4,16,16]{2,3,1,0:T(8,128)S(1)} %get-tuple-element.67), channel_id=1, source_target_pairs={{2,0},{4,2},{6,4},{8,6},{10,8},{12,10},{14,12},{0,14},{3,1},{5,3},... | collective-permute-start | bytes 49160 | tf_op jit(solution)/shard_map/ppermute | solution.py:21
  46.6 4.8 %collective-permute-start.15 = (f32[4,4,16,16]{2,3,1,0:T(8,128)S(1)}, f32[4,4,16,16]{2,3,1,0:T(8,128)S(1)}, u32[]{:S(2)}, u32[]{:S(2)}) collective-permute-start(f32[4,4,16,16]{2,3,1,0:T(8,128)S(1)} %get-tuple-element.66), channel_id=1, source_target_pairs={{2,0},{4,2},{6,4},{8,6},{10,8},{12,10},{14,12},{0,14},{3,1},{5,3},... | collective-permute-start | bytes 49160 | tf_op jit(solution)/shard_map/ppermute | solution.py:21
  51.4 2.8 %collective-permute-done.9 = f32[4,4,16,16]{2,3,1,0:T(8,128)S(1)} collective-permute-done((f32[4,4,16,16]{2,3,1,0:T(8,128)S(1)}, f32[4,4,16,16]{2,3,1,0:T(8,128)S(1)}, u32[]{:S(2)}, u32[]{:S(2)}) %collective-permute-start.9) | collective-permute-done | bytes 16416 | tf_op jit(solution)/shard_map/ppermute | solution.py:20
  54.3 1.3 %collective-permute-done.14 = f32[4,4,16,16]{2,3,1,0:T(8,128)S(1)} collective-permute-done((f32[4,4,16,16]{2,3,1,0:T(8,128)S(1)}, f32[4,4,16,16]{2,3,1,0:T(8,128)S(1)}, u32[]{:S(2)}, u32[]{:S(2)}) %collective-permute-start.14) | collective-permute-done | bytes 16416 | tf_op jit(solution)/shard_map/ppermute | solution.py:20
  55.6 1.8 %collective-permute-done.15 = f32[4,4,16,16]{2,3,1,0:T(8,128)S(1)} collective-permute-done((f32[4,4,16,16]{2,3,1,0:T(8,128)S(1)}, f32[4,4,16,16]{2,3,1,0:T(8,128)S(1)}, u32[]{:S(2)}, u32[]{:S(2)}) %collective-permute-start.15) | collective-permute-done | bytes 16416 | tf_op jit(solution)/shard_map/ppermute | solution.py:21
  59.1 0.7 copy-done.5
  59.9 0.7 reshape.210
  60.7 3.8 %all-to-all-start = ((f32[8,1,512]{2,1,0:T(1,128)}), f32[8,1,512]{2,1,0:T(1,128)S(1)}, u32[]{:S(2)}, u32[]{:S(2)}) async-start(f32[8,1,512]{2,1,0:T(1,128)} %reshape.210), calls=%async_computation | async-start | bytes 32768 | tf_op jit(solution)/shard_map/all_to_all | solution.py:173
  64.7 6.3 %all-to-all-done = f32[8,1,512]{2,1,0:T(1,128)S(1)} async-done(((f32[8,1,512]{2,1,0:T(1,128)}), f32[8,1,512]{2,1,0:T(1,128)S(1)}, u32[]{:S(2)}, u32[]{:S(2)}) %all-to-all-start) | async-done | bytes 16416 | tf_op jit(solution)/shard_map/all_to_all | solution.py:173
  76.5 0.7 reshape.212
  77.2 3.3 %all-to-all-start.1 = ((f32[8,1,512]{2,1,0:T(1,128)}), f32[8,1,512]{2,1,0:T(1,128)S(1)}, u32[]{:S(2)}, u32[]{:S(2)}) async-start(f32[8,1,512]{2,1,0:T(1,128)} %reshape.212), calls=%async_computation.1 | async-start | bytes 32768 | tf_op jit(solution)/shard_map/all_to_all | solution.py:177
  80.6 0.8 copy.173
  81.3 5.7 %all-to-all-done.1 = f32[8,1,512]{2,1,0:T(1,128)S(1)} async-done(((f32[8,1,512]{2,1,0:T(1,128)}), f32[8,1,512]{2,1,0:T(1,128)S(1)}, u32[]{:S(2)}, u32[]{:S(2)}) %all-to-all-start.1) | async-done | bytes 16416 | tf_op jit(solution)/shard_map/all_to_all | solution.py:177
  87.1 0.7 reduce.1
  88.1 0.8 copy.172
  (152 shorter events, 13.0 us)
Async XLA Ops:
  1.3 12.8 %collective-permute-start = (f32[4,16]{1,0:T(4,128)S(1)}, f32[4,16]{1,0:T(4,128)S(1)}, u32[]{:S(2)}, u32[]{:S(2)}) collective-permute-start(f32[4,16]{1,0:T(4,128)S(1)} %get-tuple-element.69), channel_id=1, source_target_pairs={{0,2},{2,4},{4,6},{6,8},{8,10},{10,12},{12,14},{14,0},{1,3},{3,5},... | collective-permute-start | bytes 776 | tf_op jit(solution)/shard_map/ppermute | solution.py:20
  4.3 15.3 %collective-permute-start.1 = (f32[4,16]{1,0:T(4,128)S(1)}, f32[4,16]{1,0:T(4,128)S(1)}, u32[]{:S(2)}, u32[]{:S(2)}) collective-permute-start(f32[4,16]{1,0:T(4,128)S(1)} %get-tuple-element.69), channel_id=1, source_target_pairs={{2,0},{4,2},{6,4},{8,6},{10,8},{12,10},{14,12},{0,14},{3,1},{5,3},... | collective-permute-start | bytes 776 | tf_op jit(solution)/shard_map/ppermute | solution.py:21
  7.3 18.2 %collective-permute-start.5 = (f32[4,16,16]{2,1,0:T(8,128)}, f32[4,16,16]{2,1,0:T(8,128)S(1)}, u32[]{:S(2)}, u32[]{:S(2)}) collective-permute-start(f32[4,16,16]{2,1,0:T(8,128)} %param.9), channel_id=1, source_target_pairs={{0,2},{2,4},{4,6},{6,8},{8,10},{10,12},{12,14},{14,0},{1,3},{3,5},... | collective-permute-start | bytes 12296 | tf_op jit(solution)/shard_map/ppermute | solution.py:20
  7.3 23.0 %collective-permute-start.6 = (f32[4,16,16]{2,1,0:T(8,128)}, f32[4,16,16]{2,1,0:T(8,128)S(1)}, u32[]{:S(2)}, u32[]{:S(2)}) collective-permute-start(f32[4,16,16]{2,1,0:T(8,128)} %param.9), channel_id=1, source_target_pairs={{2,0},{4,2},{6,4},{8,6},{10,8},{12,10},{14,12},{0,14},{3,1},{5,3},... | collective-permute-start | bytes 12296 | tf_op jit(solution)/shard_map/ppermute | solution.py:21
  12.0 18.3 %collective-permute-start.7 = (f32[4,16,16]{2,1,0:T(8,128)}, f32[4,16,16]{2,1,0:T(8,128)S(1)}, u32[]{:S(2)}, u32[]{:S(2)}) collective-permute-start(f32[4,16,16]{2,1,0:T(8,128)} %param.10), channel_id=1, source_target_pairs={{0,2},{2,4},{4,6},{6,8},{8,10},{10,12},{12,14},{14,0},{1,3},{3,5},... | collective-permute-start | bytes 12296 | tf_op jit(solution)/shard_map/ppermute | solution.py:20
  13.0 0.9 %copy-start.2 = (f32[4,4,16,16]{3,2,1,0:T(8,128)S(1)}, f32[4,4,16,16]{3,2,1,0:T(8,128)}, u32[]{:S(2)}) copy-start(f32[4,4,16,16]{3,2,1,0:T(8,128)} %param.7) | copy-start | bytes 49156
  13.1 0.7 copy-start.6
  14.0 0.8 copy-start.4
  14.8 20.3 %collective-permute-start.8 = (f32[4,16,16]{2,1,0:T(8,128)S(1)}, f32[4,16,16]{2,1,0:T(8,128)S(1)}, u32[]{:S(2)}, u32[]{:S(2)}) collective-permute-start(f32[4,16,16]{2,1,0:T(8,128)S(1)} %copy-done.4), channel_id=1, source_target_pairs={{2,0},{4,2},{6,4},{8,6},{10,8},{12,10},{14,12},{0,14},{3,1},{5,3},... | collective-permute-start | bytes 12296 | tf_op jit(solution)/shard_map/ppermute | solution.py:21
  19.5 3.1 %collective-permute-start.11 = (f32[4,1,16,16]{2,3,1,0:T(8,128)S(1)}, f32[4,1,16,16]{2,3,1,0:T(8,128)S(1)}, u32[]{:S(2)}, u32[]{:S(2)}) collective-permute-start(f32[4,1,16,16]{2,3,1,0:T(8,128)S(1)} %slice.551), channel_id=1, source_target_pairs={{1,0},{3,2},{5,4},{7,6},{9,8},{11,10},{13,12},{15,14},{17,16},{19,... | collective-permute-start | bytes 12296 | tf_op jit(solution)/shard_map/ppermute | solution.py:29
  22.6 2.9 %collective-permute-start.2 = (f32[4,1,16,16]{2,3,1,0:T(8,128)S(1)}, f32[4,1,16,16]{2,3,1,0:T(8,128)S(1)}, u32[]{:S(2)}, u32[]{:S(2)}) collective-permute-start(f32[4,1,16,16]{2,3,1,0:T(8,128)S(1)} %slice.492), channel_id=1, source_target_pairs={{0,1},{2,3},{4,5},{6,7},{8,9},{10,11},{12,13},{14,15},{16,17},{18,... | collective-permute-start | bytes 12296 | tf_op jit(solution)/shard_map/ppermute | solution.py:29
  24.7 10.4 %copy-start.3 = (f32[4,16,16]{2,1,0:T(8,128)S(1)}, f32[4,16,16]{2,1,0:T(8,128)}, u32[]{:S(2)}) copy-start(f32[4,16,16]{2,1,0:T(8,128)} %param.9) | copy-start | bytes 12292
  25.5 11.4 %collective-permute-start.12 = (f32[4,4,16,16]{2,3,1,0:T(8,128)S(1)}, f32[4,4,16,16]{2,3,1,0:T(8,128)S(1)}, u32[]{:S(2)}, u32[]{:S(2)}) collective-permute-start(f32[4,4,16,16]{2,3,1,0:T(8,128)S(1)} %pad_maximum_fusion.5), channel_id=1, source_target_pairs={{0,2},{2,4},{4,6},{6,8},{8,10},{10,12},{12,14},{14,0},{1,3},{3,5},... | collective-permute-start | bytes 49160 | tf_op jit(solution)/shard_map/ppermute | solution.py:20
  25.6 11.3 %collective-permute-start.13 = (f32[4,4,16,16]{2,3,1,0:T(8,128)S(1)}, f32[4,4,16,16]{2,3,1,0:T(8,128)S(1)}, u32[]{:S(2)}, u32[]{:S(2)}) collective-permute-start(f32[4,4,16,16]{2,3,1,0:T(8,128)S(1)} %pad_maximum_fusion.5), channel_id=1, source_target_pairs={{2,0},{4,2},{6,4},{8,6},{10,8},{12,10},{14,12},{0,14},{3,1},{5,3},... | collective-permute-start | bytes 49160 | tf_op jit(solution)/shard_map/ppermute | solution.py:21
  30.3 8.0 %collective-permute-start.3 = (f32[4,4,16,16]{2,3,1,0:T(8,128)S(1)}, f32[4,4,16,16]{2,3,1,0:T(8,128)S(1)}, u32[]{:S(2)}, u32[]{:S(2)}) collective-permute-start(f32[4,4,16,16]{2,3,1,0:T(8,128)S(1)} %pad_maximum_fusion.4), channel_id=1, source_target_pairs={{0,2},{2,4},{4,6},{6,8},{8,10},{10,12},{12,14},{14,0},{1,3},{3,5},... | collective-permute-start | bytes 49160 | tf_op jit(solution)/shard_map/ppermute | solution.py:20
  30.3 9.4 %collective-permute-start.4 = (f32[4,4,16,16]{2,3,1,0:T(8,128)S(1)}, f32[4,4,16,16]{2,3,1,0:T(8,128)S(1)}, u32[]{:S(2)}, u32[]{:S(2)}) collective-permute-start(f32[4,4,16,16]{2,3,1,0:T(8,128)S(1)} %pad_maximum_fusion.4), channel_id=1, source_target_pairs={{2,0},{4,2},{6,4},{8,6},{10,8},{12,10},{14,12},{0,14},{3,1},{5,3},... | collective-permute-start | bytes 49160 | tf_op jit(solution)/shard_map/ppermute | solution.py:21
  37.0 0.8 copy-start
  39.8 1.0 %slice-start = ((f32[12,4,16,16]{2,3,1,0:T(8,128)}), f32[10,4,16,16]{2,3,1,0:T(8,128)S(1)}, s32[]{:S(2)}) async-start(f32[12,4,16,16]{2,3,1,0:T(8,128)} %copy-done), calls=%async_computation.2 | async-start | bytes 655360 | tf_op jit(solution)/shard_map/slice | solution.py:72
  40.8 1.0 %copy-start.1 = (f32[12,4,16,16]{2,3,1,0:T(8,128)S(1)}, f32[12,4,16,16]{2,3,1,0:T(8,128)}, u32[]{:S(2)}) copy-start(f32[12,4,16,16]{2,3,1,0:T(8,128)} %copy-done) | copy-start | bytes 147460
  43.5 7.9 %collective-permute-start.10 = (f32[4,4,16,16]{2,3,1,0:T(8,128)S(1)}, f32[4,4,16,16]{2,3,1,0:T(8,128)S(1)}, u32[]{:S(2)}, u32[]{:S(2)}) collective-permute-start(f32[4,4,16,16]{2,3,1,0:T(8,128)S(1)} %get-tuple-element.67), channel_id=1, source_target_pairs={{2,0},{4,2},{6,4},{8,6},{10,8},{12,10},{14,12},{0,14},{3,1},{5,3},... | collective-permute-start | bytes 49160 | tf_op jit(solution)/shard_map/ppermute | solution.py:21
  46.5 7.7 %collective-permute-start.9 = (f32[4,4,16,16]{2,3,1,0:T(8,128)S(1)}, f32[4,4,16,16]{2,3,1,0:T(8,128)S(1)}, u32[]{:S(2)}, u32[]{:S(2)}) collective-permute-start(f32[4,4,16,16]{2,3,1,0:T(8,128)S(1)} %get-tuple-element.67), channel_id=1, source_target_pairs={{0,2},{2,4},{4,6},{6,8},{8,10},{10,12},{12,14},{14,0},{1,3},{3,5},... | collective-permute-start | bytes 49160 | tf_op jit(solution)/shard_map/ppermute | solution.py:20
  46.6 9.0 %collective-permute-start.14 = (f32[4,4,16,16]{2,3,1,0:T(8,128)S(1)}, f32[4,4,16,16]{2,3,1,0:T(8,128)S(1)}, u32[]{:S(2)}, u32[]{:S(2)}) collective-permute-start(f32[4,4,16,16]{2,3,1,0:T(8,128)S(1)} %get-tuple-element.66), channel_id=1, source_target_pairs={{0,2},{2,4},{4,6},{6,8},{8,10},{10,12},{12,14},{14,0},{1,3},{3,5},... | collective-permute-start | bytes 49160 | tf_op jit(solution)/shard_map/ppermute | solution.py:20
  46.6 10.8 %collective-permute-start.15 = (f32[4,4,16,16]{2,3,1,0:T(8,128)S(1)}, f32[4,4,16,16]{2,3,1,0:T(8,128)S(1)}, u32[]{:S(2)}, u32[]{:S(2)}) collective-permute-start(f32[4,4,16,16]{2,3,1,0:T(8,128)S(1)} %get-tuple-element.66), channel_id=1, source_target_pairs={{2,0},{4,2},{6,4},{8,6},{10,8},{12,10},{14,12},{0,14},{3,1},{5,3},... | collective-permute-start | bytes 49160 | tf_op jit(solution)/shard_map/ppermute | solution.py:21
  59.1 0.7 copy-start.5
  60.7 10.3 %all-to-all-start = ((f32[8,1,512]{2,1,0:T(1,128)}), f32[8,1,512]{2,1,0:T(1,128)S(1)}, u32[]{:S(2)}, u32[]{:S(2)}) async-start(f32[8,1,512]{2,1,0:T(1,128)} %reshape.210), calls=%async_computation | async-start | bytes 32768 | tf_op jit(solution)/shard_map/all_to_all | solution.py:173
  77.2 9.9 %all-to-all-start.1 = ((f32[8,1,512]{2,1,0:T(1,128)}), f32[8,1,512]{2,1,0:T(1,128)S(1)}, u32[]{:S(2)}, u32[]{:S(2)}) async-start(f32[8,1,512]{2,1,0:T(1,128)} %reshape.212), calls=%async_computation.1 | async-start | bytes 32768 | tf_op jit(solution)/shard_map/all_to_all | solution.py:177
where the time goes:
time: 89.4 us; the launch traced here: 88.9 us
  starting transfers between devices  43.2 us (48%)
  waiting for transfers between devices  22.6 us (25%)
  local copies, waits for them, and re-layouts  12.8 us (14%)
  other arithmetic  5.55 us (6%)
  matrix products  3.17 us (4%)
  between operations  1.5 us (2%)
    ppermute x7, starting transfers between devices, extended(): after = lax.ppermute(leading, axis, down)  29.7 us
    unnamed x24, local copies, waits for them, and re-layouts  8.26 us
    all_to_all x1, waiting for transfers between devices, body(): lax.all_to_all(weighted, 'tiles', split_axis=3, concat_axis=0, tiled=True)  6.35 us
    all_to_all x1, waiting for transfers between devices, body(): lax.all_to_all(smoothed, 'tiles', split_axis=0, concat_axis=3, tiled=True)  5.73 us
    ppermute x7, waiting for transfers between devices, extended(): before = lax.ppermute(last, axis, up)  4.73 us
    all_to_all x1, starting transfers between devices, body(): lax.all_to_all(weighted, 'tiles', split_axis=3, concat_axis=0, tiled=True)  3.77 us
    ppermute x2, starting transfers between devices, passed_along(): return lax.ppermute(x, axis, pairs)  3.34 us
    all_to_all x1, starting transfers between devices, body(): lax.all_to_all(smoothed, 'tiles', split_axis=0, concat_axis=3, tiled=True)  3.34 us
  transfers between devices with their start and end apart: 18, of which 9 were waited for; matrix products, arithmetic and copies ran while one was open for 5% of the time, Pallas kernels for 0%

commit v1 on v0

--- a/solution.py
+++ b/solution.py
@@ -1,8 +1,11 @@
+import functools
 import math
 
 import jax
 import jax.numpy as jnp
 from jax import lax
+from jax.experimental import pallas as pl
+from jax.experimental.pallas import tpu as pltpu
 from jax.sharding import PartitionSpec as P
 
 STEPS = 8
@@ -156,7 +159,7 @@
     return (smoothed / count).reshape(bands.shape)
 
 
-def body(increment, dual_vector, wind_u, wind_v, land_sea, length_sq, spread):
+def stepwise_body(increment, dual_vector, wind_u, wind_v, land_sea, length_sq, spread):
     margin = 4
     mixing = 0.15 + 0.09 * land_sea.astype(jnp.float32)
     grown_u, grown_v, grown_mix = (
@@ -179,6 +182,313 @@
     return (covar + increment - forward, dual_vector - backward)
 
 
+ROWS = 8
+LANES = 128
+MESH = pl.DeviceIdType.MESH
+
+
+def circulant_row(lengths, count):
+    half = count // 2
+    damped = []
+    for wave in range(half + 1):
+        basic = 1.0 - math.cos(2.0 * math.pi * wave / count)
+        base = 1.0 + (2.0 * basic) * lengths
+        power = base
+        for _ in range(SWEEPS - 1):
+            power = power * base
+        weight = (1.0 if wave in (0, half) else 2.0) / count
+        damped.append(weight / power)
+    row = [None] * (half + 1)
+    for distance in range(half // 2 + 1):
+        sums = [jnp.zeros_like(lengths), jnp.zeros_like(lengths)]
+        for wave in range(half + 1):
+            factor = math.cos(2.0 * math.pi * (wave * distance % count) / count)
+            sums[wave % 2] = sums[wave % 2] + factor * damped[wave]
+        row[distance] = sums[0] + sums[1]
+        row[half - distance] = sums[0] - sums[1]
+    return row
+
+
+def kernel(
+    tiles,
+    reach,
+    inc_ref,
+    dual_ref,
+    u_ref,
+    v_ref,
+    land_ref,
+    length_ref,
+    spread_ref,
+    model_out,
+    dual_out,
+    data,
+    cross,
+    other,
+    coef,
+    send_sem,
+    recv_sem,
+    cross_send,
+    cross_recv,
+):
+    lons, subs, levs, lats = inc_ref.shape
+    high = levs // ROWS
+    span = high * lats
+    bands = length_ref.shape[1]
+    me = lax.axis_index("tiles")
+    sub = lax.axis_index("subwin")
+    near = [d for d in range(1, reach + 1)] + [tiles - d for d in range(1, reach + 1)]
+    far = [d for d in range(1, tiles) if d not in near]
+    beside = list(range(-reach, reach + 1))
+
+    def at(distance):
+        return lax.rem(me + (distance + tiles), tiles)
+
+    barrier = pltpu.get_barrier_semaphore()
+    for d in near + far:
+        pl.semaphore_signal(barrier, inc=1, device_id={"tiles": at(d)}, device_id_type=MESH)
+    for d in beside:
+        pl.semaphore_signal(
+            barrier, inc=1, device_id={"tiles": at(d), "subwin": 1 - sub}, device_id_type=MESH
+        )
+
+    lane = lax.broadcasted_iota(jnp.int32, (ROWS, LANES), 1)
+    row = lax.broadcasted_iota(jnp.int32, (ROWS, LANES), 0)
+    group = lane // span
+    lat = lane % lats
+
+    def joined(pieces):
+        return jnp.concatenate(pieces, axis=1)
+
+    def turned(x, by):
+        by = by % LANES
+        return x if by == 0 else pltpu.roll(x, by, 1)
+
+    inc = [
+        joined([inc_ref[i, s, h * ROWS : (h + 1) * ROWS, :] for s in range(subs) for h in range(high)])
+        for i in range(lons)
+    ]
+    dual = [
+        joined([dual_ref[i, s, h * ROWS : (h + 1) * ROWS, :] for s in range(subs) for h in range(high)])
+        for i in range(lons)
+    ]
+    wind_u = joined([u_ref[i, h * ROWS : (h + 1) * ROWS, :] for i in range(lons) for h in range(high)])
+    wind_v = joined([v_ref[i, h * ROWS : (h + 1) * ROWS, :] for i in range(lons) for h in range(high)])
+    mixing = 0.15 + 0.09 * land_ref[...].astype(jnp.float32)
+    mixing = joined([mixing[i : i + 1] for i in range(lons) for h in range(high)])
+    lengths = jnp.zeros((ROWS, LANES), jnp.float32)
+    for s in range(subs):
+        for b in range(bands):
+            here = jnp.logical_and(group == s, lat == me * bands + b)
+            lengths = jnp.where(here, length_ref[s, b], lengths)
+    aux = jnp.where(row < ROWS // 2, lengths, jnp.broadcast_to(mixing, (ROWS, LANES)))
+    last_inc = joined(
+        [inc_ref[i, subs - 1, h * ROWS : (h + 1) * ROWS, :] for i in range(lons) for h in range(high)]
+    )
+    first_dual = joined(
+        [dual_ref[i, 0, h * ROWS : (h + 1) * ROWS, :] for i in range(lons) for h in range(high)]
+    )
+    own = inc + [wind_u, wind_v, aux] + dual
+    for n, tile in enumerate(own):
+        data[0, n * ROWS : (n + 1) * ROWS, :] = tile
+    cross[...] = jnp.where(sub == 0, last_inc, first_dual)
+
+    pl.semaphore_wait(barrier, len(near) + len(far) + len(beside))
+
+    far_from = (lons + 2) * ROWS
+    near_copies, far_copies, cross_copies = [], [], []
+    for d in near:
+        copy = pltpu.make_async_remote_copy(
+            src_ref=data.at[0],
+            dst_ref=data.at[tiles - d],
+            send_sem=send_sem.at[d],
+            recv_sem=recv_sem.at[tiles - d],
+            device_id={"tiles": at(d)},
+            device_id_type=MESH,
+        )
+        copy.start()
+        near_copies.append(copy)
+    for d in beside:
+        copy = pltpu.make_async_remote_copy(
+            src_ref=cross,
+            dst_ref=other.at[reach - d],
+            send_sem=cross_send.at[reach + d],
+            recv_sem=cross_recv.at[reach - d],
+            device_id={"tiles": at(d), "subwin": 1 - sub},
+            device_id_type=MESH,
+        )
+        copy.start()
+        cross_copies.append(copy)
+    for d in far:
+        copy = pltpu.make_async_remote_copy(
+            src_ref=data.at[0, pl.ds(far_from, (lons + 1) * ROWS)],
+            dst_ref=data.at[tiles - d, pl.ds(far_from, (lons + 1) * ROWS)],
+            send_sem=send_sem.at[d],
+            recv_sem=recv_sem.at[tiles - d],
+            device_id={"tiles": at(d)},
+            device_id_type=MESH,
+        )
+        copy.start()
+        far_copies.append(copy)
+
+    spread = jnp.zeros((ROWS, LANES), jnp.float32)
+    eye = lax.broadcasted_iota(jnp.int32, (ROWS, ROWS), 0) == lax.broadcasted_iota(
+        jnp.int32, (ROWS, ROWS), 1
+    )
+    for s in range(subs):
+        for h in range(high):
+            line = spread_ref[s : s + 1, h * ROWS : (h + 1) * ROWS]
+            column = jnp.sum(jnp.where(eye, jnp.broadcast_to(line, (ROWS, ROWS)), 0.0), 1, keepdims=True)
+            spread = jnp.where(lane // lats == s * high + h, column, spread)
+
+    for copy in near_copies + cross_copies:
+        copy.wait_recv()
+
+    def spread_out(x):
+        parts = [turned(x, q * span) for q in range(lons)]
+        outs = []
+        for i in range(lons):
+            out = parts[(0 - i) % lons]
+            for g in range(1, subs):
+                out = jnp.where(group == g, parts[(g - i) % lons], out)
+            outs.append(out)
+        return outs
+
+    up = jnp.where(sub > 0, 1.0, 0.0)
+    down = jnp.where(sub < 1, 1.0, 0.0)
+    previous, following = [], []
+    place = 0
+    for d in beside:
+        slot = d % tiles
+        us = spread_out(data[slot, lons * ROWS : (lons + 1) * ROWS, :])
+        vs = spread_out(data[slot, (lons + 1) * ROWS : (lons + 2) * ROWS, :])
+        mix = data[slot, (lons + 2) * ROWS + ROWS // 2 : (lons + 2) * ROWS + ROWS // 2 + 1, :]
+        mixes = spread_out(jnp.broadcast_to(mix, (ROWS, LANES)))
+        beyond = other[d + reach]
+        for i in range(lons):
+            at_rows = pl.ds(place * ROWS, ROWS)
+            m, u, v = mixes[i], 0.5 * us[i], 0.5 * vs[i]
+            coef[0, at_rows, :] = 1.0 - 4.0 * m
+            coef[1, at_rows, :] = m - u
+            coef[2, at_rows, :] = m + u
+            coef[3, at_rows, :] = jnp.where(lat == lats - 1, 0.0, m - v)
+            coef[4, at_rows, :] = jnp.where(lat == 0, 0.0, m + v)
+            place += 1
+            f = data[slot, i * ROWS : (i + 1) * ROWS, :]
+            g = data[slot, (lons + 3 + i) * ROWS : (lons + 4 + i) * ROWS, :]
+            previous.append(
+                jnp.where(group == 0, up * turned(beyond, -i * span), turned(f, span))
+            )
+            following.append(
+                jnp.where(
+                    group == subs - 1, down * turned(beyond, (subs - 1 - i) * span), turned(g, -span)
+                )
+            )
+    extra = reach * lons - STEPS
+    extent = place - 2 * extra
+    f = jnp.concatenate(previous[extra : place - extra], axis=0)
+    g = jnp.concatenate(following[extra : place - extra], axis=0)
+    for step in range(STEPS):
+        first = extra + step
+        count = extent - 2 * step
+        inner = pl.ds((first + 1) * ROWS, (count - 2) * ROWS)
+        lower = pl.ds(first * ROWS, (count - 2) * ROWS)
+        upper = pl.ds((first + 2) * ROWS, (count - 2) * ROWS)
+        mid = f[ROWS:-ROWS]
+        f = (
+            coef[0, inner, :] * mid
+            + coef[1, inner, :] * f[2 * ROWS :]
+            + coef[2, inner, :] * f[: -2 * ROWS]
+            + coef[3, inner, :] * turned(mid, -1)
+            + coef[4, inner, :] * turned(mid, 1)
+        )
+        mid = g[ROWS:-ROWS]
+        g = (
+            coef[0, inner, :] * mid
+            + coef[1, lower, :] * g[: -2 * ROWS]
+            + coef[2, upper, :] * g[2 * ROWS :]
+            + turned(coef[3, inner, :] * mid, 1)
+            + turned(coef[4, inner, :] * mid, -1)
+        )
+
+    for copy in far_copies:
+        copy.wait_recv()
+
+    total = jnp.zeros((1, LANES), jnp.float32)
+    for slot in range(tiles):
+        total = total + data[slot, far_from : far_from + 1, :]
+    weights = circulant_row(jnp.broadcast_to(total, (ROWS, LANES)), lons * tiles)
+    smooth = [jnp.zeros((ROWS, LANES), jnp.float32) for _ in range(lons)]
+    ring = lons * tiles
+    for slot in range(tiles):
+        for n in range(lons):
+            x = data[slot, (lons + 3 + n) * ROWS : (lons + 4 + n) * ROWS, :]
+            for i in range(lons):
+                distance = (slot * lons + n - i) % ring
+                smooth[i] = smooth[i] + weights[min(distance, ring - distance)] * x
+
+    square = spread * spread
+    for i in range(lons):
+        here = slice(i * ROWS, (i + 1) * ROWS)
+        model = square * smooth[i] + data[0, here, :] - f[here]
+        rest = data[0, (lons + 3 + i) * ROWS : (lons + 4 + i) * ROWS, :] - g[here]
+        for s in range(subs):
+            for h in range(high):
+                by = -(s * high + h) * lats
+                at_levels = slice(h * ROWS, (h + 1) * ROWS)
+                model_out[i, s, at_levels, :] = turned(model, by)[:, :lats]
+                dual_out[i, s, at_levels, :] = turned(rest, by)[:, :lats]
+
+    for copy in near_copies + cross_copies + far_copies:
+        copy.wait_send()
+
+
+def packed(tiles, subwins, increment):
+    lons, subs, levs, lats = increment.shape
+    reach = -(-STEPS // lons)
+    return (
+        subwins == 2
+        and levs % ROWS == 0
+        and subs == lons
+        and subs * (levs // ROWS) * lats == LANES
+        and 2 * reach < tiles <= 2 * ROWS
+        and lons * tiles % 4 == 0
+    )
+
+
+def direct_body(increment, dual_vector, wind_u, wind_v, land_sea, length_sq, spread):
+    tiles = lax.axis_size("tiles")
+    lons = increment.shape[0]
+    reach = -(-STEPS // lons)
+    around = 2 * reach + 1
+    vmem = pl.BlockSpec(memory_space=pltpu.VMEM)
+    smem = pl.BlockSpec(memory_space=pltpu.SMEM)
+    return pl.pallas_call(
+        functools.partial(kernel, tiles, reach),
+        out_shape=(
+            jax.ShapeDtypeStruct(increment.shape, jnp.float32),
+            jax.ShapeDtypeStruct(increment.shape, jnp.float32),
+        ),
+        in_specs=[vmem, vmem, vmem, vmem, vmem, smem, vmem],
+        out_specs=(vmem, vmem),
+        scratch_shapes=[
+            pltpu.VMEM((tiles, (2 * lons + 3) * ROWS, LANES), jnp.float32),
+            pltpu.VMEM((ROWS, LANES), jnp.float32),
+            pltpu.VMEM((around, ROWS, LANES), jnp.float32),
+            pltpu.VMEM((5, around * lons * ROWS, LANES), jnp.float32),
+            pltpu.SemaphoreType.DMA((tiles,)),
+            pltpu.SemaphoreType.DMA((tiles,)),
+            pltpu.SemaphoreType.DMA((around,)),
+            pltpu.SemaphoreType.DMA((around,)),
+        ],
+        compiler_params=pltpu.CompilerParams(collective_id=0, has_side_effects=True),
+    )(increment, dual_vector, wind_u, wind_v, land_sea, length_sq, spread)
+
+
+def body(*args):
+    fits = packed(lax.axis_size("tiles"), lax.axis_size("subwin"), args[0])
+    return direct_body(*args) if fits else stepwise_body(*args)
+
+
 def solution(mesh):
     placed = (
         P(("groups", "tiles"), "subwin", None, None),

time: 89.4 us -> 18.7 us (0.21)
  starting transfers between devices: 43.2 us -> 0 us
  waiting for transfers between devices: 22.6 us -> 0 us
  Pallas kernels: 0 us -> 14.3 us
  local copies, waits for them, and re-layouts: 12.8 us -> 3.6 us
  other arithmetic: 5.55 us -> 0 us
  matrix products: 3.17 us -> 0 us
    ppermute x16 -> x0, starting transfers between devices: 36.1 us -> none  [the longest x7 29.7 us: extended(): after = lax.ppermute(leading, axis, down)]
    pallas_call x0 -> x1, Pallas kernels: none -> 14.3 us  [direct_body(): pl.pallas_call(functools.partial(kernel, tiles, reach), out_shape=(jax.Sh...]
    all_to_all x2 -> x0, waiting for transfers between devices: 12.1 us -> none  [the longest x1 6.35 us: body(): lax.all_to_all(weighted, 'tiles', split_axis=3, concat_axis=0, tiled=True)]
    ppermute x16 -> x0, waiting for transfers between devices: 10.6 us -> none  [the longest x7 4.73 us: extended(): before = lax.ppermute(last, axis, up)]
    all_to_all x2 -> x0, starting transfers between devices: 7.1 us -> none  [the longest x1 3.77 us: body(): lax.all_to_all(weighted, 'tiles', split_axis=3, concat_axis=0, tiled=True)]
    unnamed x24 -> x5, local copies, waits for them, and re-layouts: 8.26 us -> 3.6 us
    dot_general x12 -> x0, matrix products: 3.17 us -> none  [contract(): return jnp.einsum(form, first, second, precision=lax.Precision.HIGHEST)]
    slice x62 -> x0, local copies, waits for them, and re-layouts: 2.7 us -> none  [the longest x30 1.29 us: tangent_step(): coeff[offset + 1:offset + extent - 1][:, None]]
  transfers between devices with their start and end apart: 18 -> 0, of which waited for: 9 -> 0; matrix products, arithmetic and copies ran while one was open for 5% -> 0% of each run, Pallas kernels for 0% -> 0%
where the time goes in v1:
time: 18.7 us; the launch traced here: 18.5 us
  Pallas kernels  14.3 us (76%)
  local copies, waits for them, and re-layouts  3.6 us (19%)
  between operations  0.65 us (3%)
    pallas_call x1, Pallas kernels, direct_body(): pl.pallas_call(functools.partial(kernel, tiles, reach), out_shape=(jax.Sh...  14.3 us
    unnamed x5, local copies, waits for them, and re-layouts  3.6 us

profile of v1, /device:TPU:0, one launch (start us, length us, event | category | flops | bytes accessed | tf_op | source)
XLA Modules:
  0.0 18.5 jit_solution(831718748372871918)
XLA Ops:
  0.6 1.3 %copy.9.length_ref = f32[4,2]{1,0:T(4,128)} copy(f32[4,2]{0,1:T(2,128)} %param.12) | data formatting | bytes 64 | tf_op args[5]
  2.0 14.3 %shard_map.86 = (f32[4,4,16,16]{3,2,1,0:T(8,128)}, f32[4,4,16,16]{3,2,1,0:T(8,128)}) custom-call(f32[4,4,16,16]{3,2,1,0:T(8,128)} %inc_ref.1, f32[4,4,16,16]{3,2,1,0:T(8,128)} %dual_ref.1, f32[4,16,16]{2,1,0:T(8,128)} %u_ref.1, f32[4,16,16]{2,1,0:T(8,128)} %v_ref.1, s32[4,16]{1,0:T(4,128)} %land_ref.1, f32[4,2]{1,0:T(4,128)} %copy.9.length_ref, ...), custom_call_target="tpu_custom_call" | custom-call | tf_op jit(solution)/shard_map/pallas_call | solution.py:465
  16.3 0.0 copy-start
  16.3 1.6 %copy.12 = f32[4,4,16,16]{3,2,1,0:T(8,128)} copy(f32[4,4,16,16]{3,2,1,0:T(8,128)} %get-tuple-element.4) | data formatting | bytes 32768
  17.9 0.0 copy-done
  17.9 0.7 %copy.13 = f32[4,4,16,16]{3,2,1,0:T(8,128)} copy(f32[4,4,16,16]{3,2,1,0:T(8,128)S(1)} %copy-done) | data formatting | bytes 32768
Async XLA Ops:
  16.3 1.6 %copy-start = (f32[4,4,16,16]{3,2,1,0:T(8,128)S(1)}, f32[4,4,16,16]{3,2,1,0:T(8,128)}, u32[]{:S(2)}) copy-start(f32[4,4,16,16]{3,2,1,0:T(8,128)} %get-tuple-element.5) | copy-start | bytes 49156

commit v2 on v1

--- a/solution.py
+++ b/solution.py
@@ -212,15 +212,13 @@
 def kernel(
     tiles,
     reach,
-    inc_ref,
-    dual_ref,
-    u_ref,
-    v_ref,
-    land_ref,
-    length_ref,
-    spread_ref,
-    model_out,
-    dual_out,
+    *refs,
+):
+    count = 7
+    held, packed_out = refs[:count], refs[count]
+    here_refs = refs[count + 1 : 2 * count + 1]
+    inc_ref, dual_ref, u_ref, v_ref, land_ref, length_ref, spread_ref = here_refs
+    (
     data,
     cross,
     other,
@@ -229,11 +227,17 @@
     recv_sem,
     cross_send,
     cross_recv,
-):
+    load_sem,
+    ) = refs[2 * count + 1 :]
+    loads = [
+        pltpu.make_async_copy(held[n], here_refs[n], load_sem.at[n]) for n in range(count)
+    ]
+    for load in loads:
+        load.start()
     lons, subs, levs, lats = inc_ref.shape
     high = levs // ROWS
     span = high * lats
-    bands = length_ref.shape[1]
+    bands = length_ref.shape[0]
     me = lax.axis_index("tiles")
     sub = lax.axis_index("subwin")
     near = [d for d in range(1, reach + 1)] + [tiles - d for d in range(1, reach + 1)]
@@ -263,6 +267,8 @@
         by = by % LANES
         return x if by == 0 else pltpu.roll(x, by, 1)
 
+    for load in loads:
+        load.wait()
     inc = [
         joined([inc_ref[i, s, h * ROWS : (h + 1) * ROWS, :] for s in range(subs) for h in range(high)])
         for i in range(lons)
@@ -279,7 +285,7 @@
     for s in range(subs):
         for b in range(bands):
             here = jnp.logical_and(group == s, lat == me * bands + b)
-            lengths = jnp.where(here, length_ref[s, b], lengths)
+            lengths = jnp.where(here, length_ref[b : b + 1, s : s + 1], lengths)
     aux = jnp.where(row < ROWS // 2, lengths, jnp.broadcast_to(mixing, (ROWS, LANES)))
     last_inc = joined(
         [inc_ref[i, subs - 1, h * ROWS : (h + 1) * ROWS, :] for i in range(lons) for h in range(high)]
@@ -429,20 +435,28 @@
     square = spread * spread
     for i in range(lons):
         here = slice(i * ROWS, (i + 1) * ROWS)
-        model = square * smooth[i] + data[0, here, :] - f[here]
-        rest = data[0, (lons + 3 + i) * ROWS : (lons + 4 + i) * ROWS, :] - g[here]
-        for s in range(subs):
-            for h in range(high):
-                by = -(s * high + h) * lats
-                at_levels = slice(h * ROWS, (h + 1) * ROWS)
-                model_out[i, s, at_levels, :] = turned(model, by)[:, :lats]
-                dual_out[i, s, at_levels, :] = turned(rest, by)[:, :lats]
+        packed_out[0, here, :] = square * smooth[i] + data[0, here, :] - f[here]
+        rest = data[0, (lons + 3 + i) * ROWS : (lons + 4 + i) * ROWS, :]
+        packed_out[1, here, :] = rest - g[here]
 
     for copy in near_copies + cross_copies + far_copies:
         copy.wait_send()
 
 
-def packed(tiles, subwins, increment):
+def unpack(packed_ref, model_out, dual_out):
+    lons, subs, levs, lats = model_out.shape
+    high = levs // ROWS
+    for i in range(lons):
+        for n, out in enumerate((model_out, dual_out)):
+            tile = packed_ref[n, i * ROWS : (i + 1) * ROWS, :]
+            for s in range(subs):
+                for h in range(high):
+                    by = (s * high + h) * lats
+                    moved = pltpu.roll(tile, LANES - by, 1) if by else tile
+                    out[i, s, h * ROWS : (h + 1) * ROWS, :] = moved[:, :lats]
+
+
+def fills_tiles(tiles, subwins, increment):
     lons, subs, levs, lats = increment.shape
     reach = -(-STEPS // lons)
     return (
@@ -461,16 +475,16 @@
     reach = -(-STEPS // lons)
     around = 2 * reach + 1
     vmem = pl.BlockSpec(memory_space=pltpu.VMEM)
-    smem = pl.BlockSpec(memory_space=pltpu.SMEM)
-    return pl.pallas_call(
+    hbm = pl.BlockSpec(memory_space=pltpu.HBM)
+    args = (increment, dual_vector, wind_u, wind_v, land_sea, length_sq.T, spread)
+    result = jax.ShapeDtypeStruct(increment.shape, jnp.float32)
+    packed = pl.pallas_call(
         functools.partial(kernel, tiles, reach),
-        out_shape=(
-            jax.ShapeDtypeStruct(increment.shape, jnp.float32),
-            jax.ShapeDtypeStruct(increment.shape, jnp.float32),
-        ),
-        in_specs=[vmem, vmem, vmem, vmem, vmem, smem, vmem],
-        out_specs=(vmem, vmem),
-        scratch_shapes=[
+        out_shape=jax.ShapeDtypeStruct((2, lons * ROWS, LANES), jnp.float32),
+        in_specs=[hbm] * len(args),
+        out_specs=vmem,
+        scratch_shapes=[pltpu.VMEM(x.shape, x.dtype) for x in args]
+        + [
             pltpu.VMEM((tiles, (2 * lons + 3) * ROWS, LANES), jnp.float32),
             pltpu.VMEM((ROWS, LANES), jnp.float32),
             pltpu.VMEM((around, ROWS, LANES), jnp.float32),
@@ -479,13 +493,17 @@
             pltpu.SemaphoreType.DMA((tiles,)),
             pltpu.SemaphoreType.DMA((around,)),
             pltpu.SemaphoreType.DMA((around,)),
+            pltpu.SemaphoreType.DMA((len(args),)),
         ],
         compiler_params=pltpu.CompilerParams(collective_id=0, has_side_effects=True),
-    )(increment, dual_vector, wind_u, wind_v, land_sea, length_sq, spread)
+    )(*args)
+    return pl.pallas_call(
+        unpack, out_shape=(result, result), in_specs=[vmem], out_specs=(vmem, vmem)
+    )(packed)
 
 
 def body(*args):
-    fits = packed(lax.axis_size("tiles"), lax.axis_size("subwin"), args[0])
+    fits = fills_tiles(lax.axis_size("tiles"), lax.axis_size("subwin"), args[0])
     return direct_body(*args) if fits else stepwise_body(*args)
 
 

time: 18.7 us -> 15.9 us (0.85)
  local copies, waits for them, and re-layouts: 3.6 us -> 0 us
  Pallas kernels: 14.3 us -> 15 us
    unnamed x5 -> x0, local copies, waits for them, and re-layouts: 3.6 us -> none
    pallas_call x1 -> x2, Pallas kernels: 14.3 us -> 15 us  [the longest x1 13.4 us: direct_body(): pl.pallas_call(functools.partial(kernel, tiles, reach), out_shape=jax.Sha...]
where the time goes in v2:
time: 15.9 us; the launch traced here: 15.7 us
  Pallas kernels  15 us (94%)
  between operations  0.64 us (4%)
    pallas_call x1, Pallas kernels, direct_body(): pl.pallas_call(functools.partial(kernel, tiles, reach), out_shape=jax.Sha...  13.4 us
    pallas_call x1, Pallas kernels, direct_body(): pl.pallas_call(unpack, out_shape=(result, result), in_specs=[vmem], out_s...  1.58 us

profile of v2, /device:TPU:0, one launch (start us, length us, event | category | flops | bytes accessed | tf_op | source)
XLA Modules:
  0.0 15.7 jit_solution(15000997573416002674)
XLA Ops:
  0.6 13.4 %shard_map.86.packed_ref = f32[2,32,128]{2,1,0:T(8,128)} custom-call(f32[4,4,16,16]{3,2,1,0:T(8,128)} %refs_0_.1, f32[4,4,16,16]{3,2,1,0:T(8,128)} %refs_1_.1, f32[4,16,16]{2,1,0:T(8,128)} %refs_2_.1, f32[4,16,16]{2,1,0:T(8,128)} %refs_3_.1, s32[4,16]{1,0:T(4,128)} %refs_4_.1, f32[2,4]{1,0:T(2,128)} %bitcast.1, f32[4,16]{1,0:T(4,128)} %refs_6_.1), custom_call_target="tpu_custom_call" | custom-call | tf_op jit(solution)/shard_map/pallas_call | solution.py:481
  14.1 1.6 %shard_map.87 = (f32[4,4,16,16]{3,2,1,0:T(8,128)}, f32[4,4,16,16]{3,2,1,0:T(8,128)}) custom-call(f32[2,32,128]{2,1,0:T(8,128)} %shard_map.86.packed_ref), custom_call_target="tpu_custom_call" | custom-call | tf_op jit(solution)/shard_map/pallas_call | solution.py:500

commit v3 on v2

--- a/solution.py
+++ b/solution.py
@@ -219,15 +219,23 @@
     here_refs = refs[count + 1 : 2 * count + 1]
     inc_ref, dual_ref, u_ref, v_ref, land_ref, length_ref, spread_ref = here_refs
     (
-    data,
-    cross,
-    other,
-    coef,
-    send_sem,
-    recv_sem,
-    cross_send,
-    cross_recv,
-    load_sem,
+        halo,
+        cross,
+        other,
+        coef,
+        bands_out,
+        bands_in,
+        smooth_out,
+        smooth_in,
+        halo_send,
+        halo_recv,
+        cross_send,
+        cross_recv,
+        band_send,
+        band_recv,
+        back_send,
+        back_recv,
+        load_sem,
     ) = refs[2 * count + 1 :]
     loads = [
         pltpu.make_async_copy(held[n], here_refs[n], load_sem.at[n]) for n in range(count)
@@ -237,18 +245,20 @@
     lons, subs, levs, lats = inc_ref.shape
     high = levs // ROWS
     span = high * lats
-    bands = length_ref.shape[0]
+    width = length_ref.shape[0]
+    ring = lons * tiles
+    merged = tiles // lons
     me = lax.axis_index("tiles")
     sub = lax.axis_index("subwin")
-    near = [d for d in range(1, reach + 1)] + [tiles - d for d in range(1, reach + 1)]
-    far = [d for d in range(1, tiles) if d not in near]
+    others = list(range(1, tiles))
     beside = list(range(-reach, reach + 1))
+    near = [d for d in beside if d]
 
     def at(distance):
         return lax.rem(me + (distance + tiles), tiles)
 
     barrier = pltpu.get_barrier_semaphore()
-    for d in near + far:
+    for d in others:
         pl.semaphore_signal(barrier, inc=1, device_id={"tiles": at(d)}, device_id_type=MESH)
     for d in beside:
         pl.semaphore_signal(
@@ -269,45 +279,52 @@
 
     for load in loads:
         load.wait()
-    inc = [
-        joined([inc_ref[i, s, h * ROWS : (h + 1) * ROWS, :] for s in range(subs) for h in range(high)])
-        for i in range(lons)
-    ]
-    dual = [
-        joined([dual_ref[i, s, h * ROWS : (h + 1) * ROWS, :] for s in range(subs) for h in range(high)])
-        for i in range(lons)
-    ]
-    wind_u = joined([u_ref[i, h * ROWS : (h + 1) * ROWS, :] for i in range(lons) for h in range(high)])
-    wind_v = joined([v_ref[i, h * ROWS : (h + 1) * ROWS, :] for i in range(lons) for h in range(high)])
+    def pieces(ref, *index):
+        return [ref[(*index, slice(h * ROWS, (h + 1) * ROWS), slice(None))] for h in range(high)]
+
+    inc, dual = [], []
+    for i in range(lons):
+        of_inc = [pieces(inc_ref, i, s) for s in range(subs)]
+        of_dual = [pieces(dual_ref, i, s) for s in range(subs)]
+        inc.append(joined(sum(of_inc, [])))
+        dual.append(joined(sum(of_dual, [])))
+        halo[reach, i * ROWS : (i + 1) * ROWS, :] = joined(sum(of_inc[:-1], []) + pieces(u_ref, i))
+        halo[reach, (lons + i) * ROWS : (lons + i + 1) * ROWS, :] = joined(
+            pieces(v_ref, i) + sum(of_dual[1:], [])
+        )
     mixing = 0.15 + 0.09 * land_ref[...].astype(jnp.float32)
     mixing = joined([mixing[i : i + 1] for i in range(lons) for h in range(high)])
-    lengths = jnp.zeros((ROWS, LANES), jnp.float32)
-    for s in range(subs):
-        for b in range(bands):
-            here = jnp.logical_and(group == s, lat == me * bands + b)
-            lengths = jnp.where(here, length_ref[b : b + 1, s : s + 1], lengths)
-    aux = jnp.where(row < ROWS // 2, lengths, jnp.broadcast_to(mixing, (ROWS, LANES)))
-    last_inc = joined(
-        [inc_ref[i, subs - 1, h * ROWS : (h + 1) * ROWS, :] for i in range(lons) for h in range(high)]
-    )
-    first_dual = joined(
-        [dual_ref[i, 0, h * ROWS : (h + 1) * ROWS, :] for i in range(lons) for h in range(high)]
-    )
-    own = inc + [wind_u, wind_v, aux] + dual
-    for n, tile in enumerate(own):
-        data[0, n * ROWS : (n + 1) * ROWS, :] = tile
+    halo[reach, 2 * lons * ROWS :, :] = jnp.broadcast_to(mixing, (ROWS, LANES))
+    last_inc = joined(sum([pieces(inc_ref, i, subs - 1) for i in range(lons)], []))
+    first_dual = joined(sum([pieces(dual_ref, i, 0) for i in range(lons)], []))
     cross[...] = jnp.where(sub == 0, last_inc, first_dual)
-
-    pl.semaphore_wait(barrier, len(near) + len(far) + len(beside))
-
-    far_from = (lons + 2) * ROWS
-    near_copies, far_copies, cross_copies = [], [], []
+    slot = lat // width
+    for t in range(tiles):
+        out = turned(dual[0], -width * t)
+        for i in range(1, lons):
+            out = jnp.where(slot == i, turned(dual[i], width * (i - t)), out)
+        bands_out[t] = out
+
+    pl.semaphore_wait(barrier, len(others) + len(beside))
+
+    band_copies, near_copies, cross_copies, back_copies = [], [], [], []
+    for d in others:
+        copy = pltpu.make_async_remote_copy(
+            src_ref=bands_out.at[at(d)],
+            dst_ref=bands_in.at[me],
+            send_sem=band_send.at[d],
+            recv_sem=band_recv.at[tiles - d],
+            device_id={"tiles": at(d)},
+            device_id_type=MESH,
+        )
+        copy.start()
+        band_copies.append(copy)
     for d in near:
         copy = pltpu.make_async_remote_copy(
-            src_ref=data.at[0],
-            dst_ref=data.at[tiles - d],
-            send_sem=send_sem.at[d],
-            recv_sem=recv_sem.at[tiles - d],
+            src_ref=halo.at[reach],
+            dst_ref=halo.at[reach - d],
+            send_sem=halo_send.at[reach + d],
+            recv_sem=halo_recv.at[reach - d],
             device_id={"tiles": at(d)},
             device_id_type=MESH,
         )
@@ -324,17 +341,23 @@
         )
         copy.start()
         cross_copies.append(copy)
-    for d in far:
-        copy = pltpu.make_async_remote_copy(
-            src_ref=data.at[0, pl.ds(far_from, (lons + 1) * ROWS)],
-            dst_ref=data.at[tiles - d, pl.ds(far_from, (lons + 1) * ROWS)],
-            send_sem=send_sem.at[d],
-            recv_sem=recv_sem.at[tiles - d],
-            device_id={"tiles": at(d)},
-            device_id_type=MESH,
-        )
-        copy.start()
-        far_copies.append(copy)
+    bands_in[pl.ds(me, 1)] = bands_out[pl.ds(me, 1)]
+
+    lengths = jnp.zeros((ROWS, LANES), jnp.float32)
+    for s in range(subs):
+        for b in range(width):
+            here = jnp.logical_and(group == s, lane % width == b)
+            lengths = jnp.where(here, length_ref[b : b + 1, s : s + 1], lengths)
+    weights = circulant_row(lengths, ring)
+
+    def weight(distance):
+        distance = distance % ring
+        return weights[min(distance, ring - distance)]
+
+    turned_weights = [
+        [jnp.where(slot >= r, weight(tiles * k + r), weight(tiles * k + r - tiles)) for r in range(tiles)]
+        for k in range(lons)
+    ]
 
     spread = jnp.zeros((ROWS, LANES), jnp.float32)
     eye = lax.broadcasted_iota(jnp.int32, (ROWS, ROWS), 0) == lax.broadcasted_iota(
@@ -345,6 +368,34 @@
             line = spread_ref[s : s + 1, h * ROWS : (h + 1) * ROWS]
             column = jnp.sum(jnp.where(eye, jnp.broadcast_to(line, (ROWS, ROWS)), 0.0), 1, keepdims=True)
             spread = jnp.where(lane // lats == s * high + h, column, spread)
+
+    for copy in band_copies:
+        copy.wait_recv()
+    sums = [jnp.zeros((ROWS, LANES), jnp.float32) for _ in range(lons)]
+    for m in range(lons):
+        x = bands_in[m * merged]
+        for p in range(1, merged):
+            x = jnp.where(slot // lons == p, turned(bands_in[m * merged + p], p * lons * width), x)
+        for r in range(tiles):
+            moved = x
+            if r:
+                moved = jnp.where(slot >= r, turned(x, r * width), turned(x, r * width - lats))
+            for n in range(lons):
+                sums[n] = sums[n] + turned_weights[(n - m) % lons][r] * moved
+    for n in range(lons):
+        smooth_out[n] = sums[n]
+    for d in others:
+        copy = pltpu.make_async_remote_copy(
+            src_ref=smooth_out.at[lax.div(at(d), merged)],
+            dst_ref=smooth_in.at[me],
+            send_sem=back_send.at[d],
+            recv_sem=back_recv.at[tiles - d],
+            device_id={"tiles": at(d)},
+            device_id_type=MESH,
+        )
+        copy.start()
+        back_copies.append(copy)
+    smooth_in[pl.ds(me, 1)] = smooth_out[pl.ds(lax.div(me, merged), 1)]
 
     for copy in near_copies + cross_copies:
         copy.wait_recv()
@@ -359,28 +410,34 @@
             outs.append(out)
         return outs
 
+    def to_all(x, g):
+        x = jnp.where(group == g, x, 0.0)
+        outs = x
+        by = 1
+        while by < subs:
+            outs = outs + turned(outs, by * span)
+            by *= 2
+        return outs
+
     up = jnp.where(sub > 0, 1.0, 0.0)
     down = jnp.where(sub < 1, 1.0, 0.0)
     previous, following = [], []
     place = 0
     for d in beside:
-        slot = d % tiles
-        us = spread_out(data[slot, lons * ROWS : (lons + 1) * ROWS, :])
-        vs = spread_out(data[slot, (lons + 1) * ROWS : (lons + 2) * ROWS, :])
-        mix = data[slot, (lons + 2) * ROWS + ROWS // 2 : (lons + 2) * ROWS + ROWS // 2 + 1, :]
-        mixes = spread_out(jnp.broadcast_to(mix, (ROWS, LANES)))
+        at_tile = d + reach
+        mixes = spread_out(halo[at_tile, 2 * lons * ROWS :, :])
         beyond = other[d + reach]
         for i in range(lons):
             at_rows = pl.ds(place * ROWS, ROWS)
-            m, u, v = mixes[i], 0.5 * us[i], 0.5 * vs[i]
+            f = halo[at_tile, i * ROWS : (i + 1) * ROWS, :]
+            g = halo[at_tile, (lons + i) * ROWS : (lons + i + 1) * ROWS, :]
+            m, u, v = mixes[i], 0.5 * to_all(f, subs - 1), 0.5 * to_all(g, 0)
             coef[0, at_rows, :] = 1.0 - 4.0 * m
             coef[1, at_rows, :] = m - u
             coef[2, at_rows, :] = m + u
             coef[3, at_rows, :] = jnp.where(lat == lats - 1, 0.0, m - v)
             coef[4, at_rows, :] = jnp.where(lat == 0, 0.0, m + v)
             place += 1
-            f = data[slot, i * ROWS : (i + 1) * ROWS, :]
-            g = data[slot, (lons + 3 + i) * ROWS : (lons + 4 + i) * ROWS, :]
             previous.append(
                 jnp.where(group == 0, up * turned(beyond, -i * span), turned(f, span))
             )
@@ -416,30 +473,26 @@
             + turned(coef[4, inner, :] * mid, -1)
         )
 
-    for copy in far_copies:
+    for copy in back_copies:
         copy.wait_recv()
-
-    total = jnp.zeros((1, LANES), jnp.float32)
-    for slot in range(tiles):
-        total = total + data[slot, far_from : far_from + 1, :]
-    weights = circulant_row(jnp.broadcast_to(total, (ROWS, LANES)), lons * tiles)
-    smooth = [jnp.zeros((ROWS, LANES), jnp.float32) for _ in range(lons)]
-    ring = lons * tiles
-    for slot in range(tiles):
-        for n in range(lons):
-            x = data[slot, (lons + 3 + n) * ROWS : (lons + 4 + n) * ROWS, :]
-            for i in range(lons):
-                distance = (slot * lons + n - i) % ring
-                smooth[i] = smooth[i] + weights[min(distance, ring - distance)] * x
-
+    own_part = lax.rem(me, merged)
+    returned = []
+    for t in range(tiles):
+        x = smooth_in[t]
+        out = x
+        for p in range(1, merged):
+            out = jnp.where(own_part == p, turned(x, -p * lons * width), out)
+        returned.append(out)
     square = spread * spread
     for i in range(lons):
         here = slice(i * ROWS, (i + 1) * ROWS)
-        packed_out[0, here, :] = square * smooth[i] + data[0, here, :] - f[here]
-        rest = data[0, (lons + 3 + i) * ROWS : (lons + 4 + i) * ROWS, :]
-        packed_out[1, here, :] = rest - g[here]
-
-    for copy in near_copies + cross_copies + far_copies:
+        smooth = turned(returned[0], -i * width)
+        for t in range(1, tiles):
+            smooth = jnp.where(slot == t, turned(returned[t], (t - i) * width), smooth)
+        packed_out[0, here, :] = square * smooth + inc[i] - f[here]
+        packed_out[1, here, :] = dual[i] - g[here]
+
+    for copy in band_copies + near_copies + cross_copies + back_copies:
         copy.wait_send()
 
 
@@ -465,7 +518,9 @@
         and subs == lons
         and subs * (levs // ROWS) * lats == LANES
         and 2 * reach < tiles <= 2 * ROWS
-        and lons * tiles % 4 == 0
+        and tiles % lons == 0
+        and lats % tiles == 0
+        and lons & (lons - 1) == 0
     )
 
 
@@ -485,14 +540,17 @@
         out_specs=vmem,
         scratch_shapes=[pltpu.VMEM(x.shape, x.dtype) for x in args]
         + [
-            pltpu.VMEM((tiles, (2 * lons + 3) * ROWS, LANES), jnp.float32),
+            pltpu.VMEM((around, (2 * lons + 1) * ROWS, LANES), jnp.float32),
             pltpu.VMEM((ROWS, LANES), jnp.float32),
             pltpu.VMEM((around, ROWS, LANES), jnp.float32),
             pltpu.VMEM((5, around * lons * ROWS, LANES), jnp.float32),
-            pltpu.SemaphoreType.DMA((tiles,)),
-            pltpu.SemaphoreType.DMA((tiles,)),
-            pltpu.SemaphoreType.DMA((around,)),
-            pltpu.SemaphoreType.DMA((around,)),
+            pltpu.VMEM((tiles, ROWS, LANES), jnp.float32),
+            pltpu.VMEM((tiles, ROWS, LANES), jnp.float32),
+            pltpu.VMEM((lons, ROWS, LANES), jnp.float32),
+            pltpu.VMEM((tiles, ROWS, LANES), jnp.float32),
+        ]
+        + [pltpu.SemaphoreType.DMA((size,)) for size in (around,) * 4 + (tiles,) * 4]
+        + [
             pltpu.SemaphoreType.DMA((len(args),)),
         ],
         compiler_params=pltpu.CompilerParams(collective_id=0, has_side_effects=True),

time: 15.9 us -> 18.3 us (1.15)
  Pallas kernels: 15 us -> 17.5 us
    pallas_call x1, Pallas kernels: 13.4 us -> 15.9 us  [direct_body(): pl.pallas_call(functools.partial(kernel, tiles, reach), out_shape=jax.Sha...]
where the time goes in v3:
time: 18.3 us; the launch traced here: 18.1 us
  Pallas kernels  17.5 us (96%)
  between operations  0.64 us (3%)
    pallas_call x1, Pallas kernels, direct_body(): pl.pallas_call(functools.partial(kernel, tiles, reach), out_shape=jax.Sha...  15.9 us
    pallas_call x1, Pallas kernels, direct_body(): pl.pallas_call(unpack, out_shape=(result, result), in_specs=[vmem], out_s...  1.58 us

profile of v3, /device:TPU:0, one launch (start us, length us, event | category | flops | bytes accessed | tf_op | source)
XLA Modules:
  0.0 18.1 jit_solution(15717802282097682438)
XLA Ops:
  0.6 15.9 %shard_map.86.packed_ref = f32[2,32,128]{2,1,0:T(8,128)} custom-call(f32[4,4,16,16]{3,2,1,0:T(8,128)} %refs_0_.1, f32[4,4,16,16]{3,2,1,0:T(8,128)} %refs_1_.1, f32[4,16,16]{2,1,0:T(8,128)} %refs_2_.1, f32[4,16,16]{2,1,0:T(8,128)} %refs_3_.1, s32[4,16]{1,0:T(4,128)} %refs_4_.1, f32[2,4]{1,0:T(2,128)} %bitcast.1, f32[4,16]{1,0:T(4,128)} %refs_6_.1), custom_call_target="tpu_custom_call" | custom-call | tf_op jit(solution)/shard_map/pallas_call | solution.py:536
  16.5 1.6 %shard_map.87 = (f32[4,4,16,16]{3,2,1,0:T(8,128)}, f32[4,4,16,16]{3,2,1,0:T(8,128)}) custom-call(f32[2,32,128]{2,1,0:T(8,128)} %shard_map.86.packed_ref), custom_call_target="tpu_custom_call" | custom-call | tf_op jit(solution)/shard_map/pallas_call | solution.py:558

commit v4 on v2

--- a/solution.py
+++ b/solution.py
@@ -220,11 +220,14 @@
     inc_ref, dual_ref, u_ref, v_ref, land_ref, length_ref, spread_ref = here_refs
     (
     data,
+    rows,
     cross,
     other,
     coef,
     send_sem,
     recv_sem,
+    row_send,
+    row_recv,
     cross_send,
     cross_recv,
     load_sem,
@@ -277,7 +280,6 @@
         joined([dual_ref[i, s, h * ROWS : (h + 1) * ROWS, :] for s in range(subs) for h in range(high)])
         for i in range(lons)
     ]
-    wind_u = joined([u_ref[i, h * ROWS : (h + 1) * ROWS, :] for i in range(lons) for h in range(high)])
     wind_v = joined([v_ref[i, h * ROWS : (h + 1) * ROWS, :] for i in range(lons) for h in range(high)])
     mixing = 0.15 + 0.09 * land_ref[...].astype(jnp.float32)
     mixing = joined([mixing[i : i + 1] for i in range(lons) for h in range(high)])
@@ -286,22 +288,41 @@
         for b in range(bands):
             here = jnp.logical_and(group == s, lat == me * bands + b)
             lengths = jnp.where(here, length_ref[b : b + 1, s : s + 1], lengths)
-    aux = jnp.where(row < ROWS // 2, lengths, jnp.broadcast_to(mixing, (ROWS, LANES)))
+    rows[0, 0:1, :] = lengths[:1]
+    rows[0, 1:2, :] = mixing
     last_inc = joined(
         [inc_ref[i, subs - 1, h * ROWS : (h + 1) * ROWS, :] for i in range(lons) for h in range(high)]
     )
     first_dual = joined(
         [dual_ref[i, 0, h * ROWS : (h + 1) * ROWS, :] for i in range(lons) for h in range(high)]
     )
-    own = inc + [wind_u, wind_v, aux] + dual
+    inc_u = [
+        joined(
+            [inc_ref[i, s, h * ROWS : (h + 1) * ROWS, :] for s in range(subs - 1) for h in range(high)]
+            + [u_ref[i, h * ROWS : (h + 1) * ROWS, :] for h in range(high)]
+        )
+        for i in range(lons)
+    ]
+    own = inc_u + [wind_v] + dual
     for n, tile in enumerate(own):
         data[0, n * ROWS : (n + 1) * ROWS, :] = tile
     cross[...] = jnp.where(sub == 0, last_inc, first_dual)
 
     pl.semaphore_wait(barrier, len(near) + len(far) + len(beside))
 
-    far_from = (lons + 2) * ROWS
-    near_copies, far_copies, cross_copies = [], [], []
+    far_from = (lons + 1) * ROWS
+    near_copies, far_copies, cross_copies, row_copies = [], [], [], []
+    for d in near + far:
+        copy = pltpu.make_async_remote_copy(
+            src_ref=rows.at[0],
+            dst_ref=rows.at[tiles - d],
+            send_sem=row_send.at[d],
+            recv_sem=row_recv.at[tiles - d],
+            device_id={"tiles": at(d)},
+            device_id_type=MESH,
+        )
+        copy.start()
+        row_copies.append(copy)
     for d in near:
         copy = pltpu.make_async_remote_copy(
             src_ref=data.at[0],
@@ -326,8 +347,8 @@
         cross_copies.append(copy)
     for d in far:
         copy = pltpu.make_async_remote_copy(
-            src_ref=data.at[0, pl.ds(far_from, (lons + 1) * ROWS)],
-            dst_ref=data.at[tiles - d, pl.ds(far_from, (lons + 1) * ROWS)],
+            src_ref=data.at[0, pl.ds(far_from, lons * ROWS)],
+            dst_ref=data.at[tiles - d, pl.ds(far_from, lons * ROWS)],
             send_sem=send_sem.at[d],
             recv_sem=recv_sem.at[tiles - d],
             device_id={"tiles": at(d)},
@@ -345,6 +366,13 @@
             line = spread_ref[s : s + 1, h * ROWS : (h + 1) * ROWS]
             column = jnp.sum(jnp.where(eye, jnp.broadcast_to(line, (ROWS, ROWS)), 0.0), 1, keepdims=True)
             spread = jnp.where(lane // lats == s * high + h, column, spread)
+
+    for copy in row_copies:
+        copy.wait_recv()
+    total = jnp.zeros((1, LANES), jnp.float32)
+    for slot in range(tiles):
+        total = total + rows[slot, 0:1, :]
+    weights = circulant_row(jnp.broadcast_to(total, (ROWS, LANES)), lons * tiles)
 
     for copy in near_copies + cross_copies:
         copy.wait_recv()
@@ -359,28 +387,34 @@
             outs.append(out)
         return outs
 
+    def to_all(x, g):
+        outs = jnp.where(group == g, x, 0.0)
+        by = 1
+        while by < subs:
+            outs = outs + turned(outs, by * span)
+            by *= 2
+        return outs
+
     up = jnp.where(sub > 0, 1.0, 0.0)
     down = jnp.where(sub < 1, 1.0, 0.0)
     previous, following = [], []
     place = 0
     for d in beside:
         slot = d % tiles
-        us = spread_out(data[slot, lons * ROWS : (lons + 1) * ROWS, :])
-        vs = spread_out(data[slot, (lons + 1) * ROWS : (lons + 2) * ROWS, :])
-        mix = data[slot, (lons + 2) * ROWS + ROWS // 2 : (lons + 2) * ROWS + ROWS // 2 + 1, :]
-        mixes = spread_out(jnp.broadcast_to(mix, (ROWS, LANES)))
+        vs = spread_out(data[slot, lons * ROWS : (lons + 1) * ROWS, :])
+        mixes = spread_out(jnp.broadcast_to(rows[slot, 1:2, :], (ROWS, LANES)))
         beyond = other[d + reach]
         for i in range(lons):
             at_rows = pl.ds(place * ROWS, ROWS)
-            m, u, v = mixes[i], 0.5 * us[i], 0.5 * vs[i]
+            f = data[slot, i * ROWS : (i + 1) * ROWS, :]
+            m, u, v = mixes[i], 0.5 * to_all(f, subs - 1), 0.5 * vs[i]
             coef[0, at_rows, :] = 1.0 - 4.0 * m
             coef[1, at_rows, :] = m - u
             coef[2, at_rows, :] = m + u
             coef[3, at_rows, :] = jnp.where(lat == lats - 1, 0.0, m - v)
             coef[4, at_rows, :] = jnp.where(lat == 0, 0.0, m + v)
             place += 1
-            f = data[slot, i * ROWS : (i + 1) * ROWS, :]
-            g = data[slot, (lons + 3 + i) * ROWS : (lons + 4 + i) * ROWS, :]
+            g = data[slot, (lons + 1 + i) * ROWS : (lons + 2 + i) * ROWS, :]
             previous.append(
                 jnp.where(group == 0, up * turned(beyond, -i * span), turned(f, span))
             )
@@ -419,15 +453,11 @@
     for copy in far_copies:
         copy.wait_recv()
 
-    total = jnp.zeros((1, LANES), jnp.float32)
-    for slot in range(tiles):
-        total = total + data[slot, far_from : far_from + 1, :]
-    weights = circulant_row(jnp.broadcast_to(total, (ROWS, LANES)), lons * tiles)
     smooth = [jnp.zeros((ROWS, LANES), jnp.float32) for _ in range(lons)]
     ring = lons * tiles
     for slot in range(tiles):
         for n in range(lons):
-            x = data[slot, (lons + 3 + n) * ROWS : (lons + 4 + n) * ROWS, :]
+            x = data[slot, (lons + 1 + n) * ROWS : (lons + 2 + n) * ROWS, :]
             for i in range(lons):
                 distance = (slot * lons + n - i) % ring
                 smooth[i] = smooth[i] + weights[min(distance, ring - distance)] * x
@@ -435,11 +465,11 @@
     square = spread * spread
     for i in range(lons):
         here = slice(i * ROWS, (i + 1) * ROWS)
-        packed_out[0, here, :] = square * smooth[i] + data[0, here, :] - f[here]
-        rest = data[0, (lons + 3 + i) * ROWS : (lons + 4 + i) * ROWS, :]
+        packed_out[0, here, :] = square * smooth[i] + inc[i] - f[here]
+        rest = data[0, (lons + 1 + i) * ROWS : (lons + 2 + i) * ROWS, :]
         packed_out[1, here, :] = rest - g[here]
 
-    for copy in near_copies + cross_copies + far_copies:
+    for copy in row_copies + near_copies + cross_copies + far_copies:
         copy.wait_send()
 
 
@@ -466,6 +496,7 @@
         and subs * (levs // ROWS) * lats == LANES
         and 2 * reach < tiles <= 2 * ROWS
         and lons * tiles % 4 == 0
+        and subs & (subs - 1) == 0
     )
 
 
@@ -480,15 +511,18 @@
     result = jax.ShapeDtypeStruct(increment.shape, jnp.float32)
     packed = pl.pallas_call(
         functools.partial(kernel, tiles, reach),
-        out_shape=jax.ShapeDtypeStruct((2, lons * ROWS, LANES), jnp.float32),
+        out_shape=pltpu.VMEM((2, lons * ROWS, LANES), jnp.float32),
         in_specs=[hbm] * len(args),
         out_specs=vmem,
         scratch_shapes=[pltpu.VMEM(x.shape, x.dtype) for x in args]
         + [
-            pltpu.VMEM((tiles, (2 * lons + 3) * ROWS, LANES), jnp.float32),
+            pltpu.VMEM((tiles, (2 * lons + 1) * ROWS, LANES), jnp.float32),
+            pltpu.VMEM((tiles, 2, LANES), jnp.float32),
             pltpu.VMEM((ROWS, LANES), jnp.float32),
             pltpu.VMEM((around, ROWS, LANES), jnp.float32),
             pltpu.VMEM((5, around * lons * ROWS, LANES), jnp.float32),
+            pltpu.SemaphoreType.DMA((tiles,)),
+            pltpu.SemaphoreType.DMA((tiles,)),
             pltpu.SemaphoreType.DMA((tiles,)),
             pltpu.SemaphoreType.DMA((tiles,)),
             pltpu.SemaphoreType.DMA((around,)),

time: 15.9 us -> 15.5 us (0.975)
  Pallas kernels: 15 us -> 13.9 us
  local copies, waits for them, and re-layouts: 0 us -> 0.61 us
    pallas_call x1, Pallas kernels: 13.4 us -> 12.3 us  [direct_body(): pl.pallas_call(functools.partial(kernel, tiles, reach), out_shape=pltpu.V...]
    unnamed x0 -> x2, local copies, waits for them, and re-layouts: none -> 0.61 us
where the time goes in v4:
time: 15.5 us; the launch traced here: 15.2 us
  Pallas kernels  13.9 us (90%)
  between operations  0.65 us (4%)
  local copies, waits for them, and re-layouts  0.61 us (4%)
    pallas_call x1, Pallas kernels, direct_body(): pl.pallas_call(functools.partial(kernel, tiles, reach), out_shape=pltpu.V...  12.3 us
    pallas_call x1, Pallas kernels, direct_body(): pl.pallas_call(unpack, out_shape=(result, result), in_specs=[vmem], out_s...  1.57 us
    unnamed x2, local copies, waits for them, and re-layouts  0.61 us

profile of v4, /device:TPU:0, one launch (start us, length us, event | category | flops | bytes accessed | tf_op | source)
XLA Modules:
  0.0 15.2 jit_solution(16710420528254793931)
XLA Ops:
  0.6 12.3 %shard_map.86.packed_ref = f32[2,32,128]{2,1,0:T(8,128)S(1)} custom-call(f32[4,4,16,16]{3,2,1,0:T(8,128)} %refs_0_.1, f32[4,4,16,16]{3,2,1,0:T(8,128)} %refs_1_.1, f32[4,16,16]{2,1,0:T(8,128)} %refs_2_.1, f32[4,16,16]{2,1,0:T(8,128)} %refs_3_.1, s32[4,16]{1,0:T(4,128)} %refs_4_.1, f32[2,4]{1,0:T(2,128)} %bitcast.1, f32[4,16]{1,0:T(4,128)} %refs_6_.1), custom_call_target="tpu_custom_call" | custom-call | tf_op jit(solution)/shard_map/pallas_call | solution.py:512
  13.0 0.0 copy-start
  13.0 0.6 %copy-done = f32[2,32,128]{2,1,0:T(8,128)} copy-done((f32[2,32,128]{2,1,0:T(8,128)}, f32[2,32,128]{2,1,0:T(8,128)S(1)}, u32[]{:S(2)}) %copy-start) | copy-done | bytes 32792
  13.6 1.6 %shard_map.87 = (f32[4,4,16,16]{3,2,1,0:T(8,128)}, f32[4,4,16,16]{3,2,1,0:T(8,128)}) custom-call(f32[2,32,128]{2,1,0:T(8,128)} %copy-done), custom_call_target="tpu_custom_call" | custom-call | tf_op jit(solution)/shard_map/pallas_call | solution.py:534
Async XLA Ops:
  13.0 0.6 %copy-start = (f32[2,32,128]{2,1,0:T(8,128)}, f32[2,32,128]{2,1,0:T(8,128)S(1)}, u32[]{:S(2)}) copy-start(f32[2,32,128]{2,1,0:T(8,128)S(1)} %shard_map.86.packed_ref) | copy-start | bytes 98308

commit v5 on v4

--- a/solution.py
+++ b/solution.py
@@ -259,7 +259,6 @@
         )
 
     lane = lax.broadcasted_iota(jnp.int32, (ROWS, LANES), 1)
-    row = lax.broadcasted_iota(jnp.int32, (ROWS, LANES), 0)
     group = lane // span
     lat = lane % lats
 
@@ -272,10 +271,6 @@
 
     for load in loads:
         load.wait()
-    inc = [
-        joined([inc_ref[i, s, h * ROWS : (h + 1) * ROWS, :] for s in range(subs) for h in range(high)])
-        for i in range(lons)
-    ]
     dual = [
         joined([dual_ref[i, s, h * ROWS : (h + 1) * ROWS, :] for s in range(subs) for h in range(high)])
         for i in range(lons)
@@ -356,6 +351,11 @@
         )
         copy.start()
         far_copies.append(copy)
+
+    inc = [
+        joined([inc_ref[i, s, h * ROWS : (h + 1) * ROWS, :] for s in range(subs) for h in range(high)])
+        for i in range(lons)
+    ]
 
     spread = jnp.zeros((ROWS, LANES), jnp.float32)
     eye = lax.broadcasted_iota(jnp.int32, (ROWS, ROWS), 0) == lax.broadcasted_iota(
@@ -450,12 +450,11 @@
             + turned(coef[4, inner, :] * mid, -1)
         )
 
-    for copy in far_copies:
-        copy.wait_recv()
-
     smooth = [jnp.zeros((ROWS, LANES), jnp.float32) for _ in range(lons)]
     ring = lons * tiles
-    for slot in range(tiles):
+    for slot in [0] + near + far:
+        if slot in far:
+            far_copies[far.index(tiles - slot)].wait_recv()
         for n in range(lons):
             x = data[slot, (lons + 1 + n) * ROWS : (lons + 2 + n) * ROWS, :]
             for i in range(lons):
@@ -532,7 +531,11 @@
         compiler_params=pltpu.CompilerParams(collective_id=0, has_side_effects=True),
     )(*args)
     return pl.pallas_call(
-        unpack, out_shape=(result, result), in_specs=[vmem], out_specs=(vmem, vmem)
+        unpack,
+        out_shape=(result, result),
+        in_specs=[vmem],
+        out_specs=(vmem, vmem),
+        compiler_params=pltpu.CompilerParams(vmem_limit_bytes=2 * 2**20),
     )(packed)
 
 

time: 15.5 us -> 14 us (0.903)
  Pallas kernels: 13.9 us -> 13.1 us
  local copies, waits for them, and re-layouts: 0.61 us -> 0 us
    pallas_call x1, Pallas kernels: 1.57 us -> 0.82 us  [direct_body(): pl.pallas_call(unpack, out_shape=(result, result), in_specs=[vmem], out_s...]
    unnamed x2 -> x0, local copies, waits for them, and re-layouts: 0.61 us -> none
where the time goes in v5:
time: 14 us; the launch traced here: 13.7 us
  Pallas kernels  13.1 us (94%)
  between operations  0.64 us (5%)
    pallas_call x1, Pallas kernels, direct_body(): pl.pallas_call(functools.partial(kernel, tiles, reach), out_shape=pltpu.V...  12.3 us
    pallas_call x1, Pallas kernels, direct_body(): pl.pallas_call(unpack, out_shape=(result, result), in_specs=[vmem], out_s...  0.82 us

profile of v5, /device:TPU:0, one launch (start us, length us, event | category | flops | bytes accessed | tf_op | source)
XLA Modules:
  0.0 13.7 jit_solution(1973811992091204143)
XLA Ops:
  0.6 12.3 %shard_map.86.packed_ref = f32[2,32,128]{2,1,0:T(8,128)S(1)} custom-call(f32[4,4,16,16]{3,2,1,0:T(8,128)} %refs_0_.1, f32[4,4,16,16]{3,2,1,0:T(8,128)} %refs_1_.1, f32[4,16,16]{2,1,0:T(8,128)} %refs_2_.1, f32[4,16,16]{2,1,0:T(8,128)} %refs_3_.1, s32[4,16]{1,0:T(4,128)} %refs_4_.1, f32[2,4]{1,0:T(2,128)} %bitcast.1, f32[4,16]{1,0:T(4,128)} %refs_6_.1), custom_call_target="tpu_custom_call" | custom-call | tf_op jit(solution)/shard_map/pallas_call | solution.py:511
  12.9 0.8 %shard_map.87 = (f32[4,4,16,16]{3,2,1,0:T(8,128)}, f32[4,4,16,16]{3,2,1,0:T(8,128)}) custom-call(f32[2,32,128]{2,1,0:T(8,128)S(1)} %shard_map.86.packed_ref), custom_call_target="tpu_custom_call" | custom-call | tf_op jit(solution)/shard_map/pallas_call | solution.py:533

commit v6 on v5

--- a/solution.py
+++ b/solution.py
@@ -306,7 +306,7 @@
     pl.semaphore_wait(barrier, len(near) + len(far) + len(beside))
 
     far_from = (lons + 1) * ROWS
-    near_copies, far_copies, cross_copies, row_copies = [], [], [], []
+    far_copies, cross_copies, row_copies = [], [], []
     for d in near + far:
         copy = pltpu.make_async_remote_copy(
             src_ref=rows.at[0],
@@ -318,17 +318,6 @@
         )
         copy.start()
         row_copies.append(copy)
-    for d in near:
-        copy = pltpu.make_async_remote_copy(
-            src_ref=data.at[0],
-            dst_ref=data.at[tiles - d],
-            send_sem=send_sem.at[d],
-            recv_sem=recv_sem.at[tiles - d],
-            device_id={"tiles": at(d)},
-            device_id_type=MESH,
-        )
-        copy.start()
-        near_copies.append(copy)
     for d in beside:
         copy = pltpu.make_async_remote_copy(
             src_ref=cross,
@@ -340,6 +329,23 @@
         )
         copy.start()
         cross_copies.append(copy)
+    outward = jnp.where(2 * me < tiles, -1, 1)
+
+    def near_copy(d):
+        slot = lax.rem(tiles - d, tiles)
+        return pltpu.make_async_remote_copy(
+            src_ref=data.at[0],
+            dst_ref=data.at[slot],
+            send_sem=send_sem.at[lax.rem(d + tiles, tiles)],
+            recv_sem=recv_sem.at[slot],
+            device_id={"tiles": at(d)},
+            device_id_type=MESH,
+        )
+
+    for side in (outward, -outward):
+        for d in range(reach, 0, -1):
+            near_copy(side * d).start()
+    near_copies = [near_copy(d) for d in near]
     for d in far:
         copy = pltpu.make_async_remote_copy(
             src_ref=data.at[0, pl.ds(far_from, lons * ROWS)],

time: 14 us -> 14.1 us (level)
  Pallas kernels: 13.1 us -> 13.3 us
    pallas_call x1, Pallas kernels: 12.3 us -> 12.5 us  [direct_body(): pl.pallas_call(functools.partial(kernel, tiles, reach), out_shape=pltpu.V...]
where the time goes in v6:
time: 14.1 us; the launch traced here: 13.9 us
  Pallas kernels  13.3 us (94%)
  between operations  0.64 us (5%)
    pallas_call x1, Pallas kernels, direct_body(): pl.pallas_call(functools.partial(kernel, tiles, reach), out_shape=pltpu.V...  12.5 us
    pallas_call x1, Pallas kernels, direct_body(): pl.pallas_call(unpack, out_shape=(result, result), in_specs=[vmem], out_s...  0.82 us

profile of v6, /device:TPU:0, one launch (start us, length us, event | category | flops | bytes accessed | tf_op | source)
XLA Modules:
  0.0 13.9 jit_solution(5358333546824670905)
XLA Ops:
  0.6 12.5 %shard_map.86.packed_ref = f32[2,32,128]{2,1,0:T(8,128)S(1)} custom-call(f32[4,4,16,16]{3,2,1,0:T(8,128)} %refs_0_.1, f32[4,4,16,16]{3,2,1,0:T(8,128)} %refs_1_.1, f32[4,16,16]{2,1,0:T(8,128)} %refs_2_.1, f32[4,16,16]{2,1,0:T(8,128)} %refs_3_.1, s32[4,16]{1,0:T(4,128)} %refs_4_.1, f32[2,4]{1,0:T(2,128)} %bitcast.1, f32[4,16]{1,0:T(4,128)} %refs_6_.1), custom_call_target="tpu_custom_call" | custom-call | tf_op jit(solution)/shard_map/pallas_call | solution.py:517
  13.1 0.8 %shard_map.87 = (f32[4,4,16,16]{3,2,1,0:T(8,128)}, f32[4,4,16,16]{3,2,1,0:T(8,128)}) custom-call(f32[2,32,128]{2,1,0:T(8,128)S(1)} %shard_map.86.packed_ref), custom_call_target="tpu_custom_call" | custom-call | tf_op jit(solution)/shard_map/pallas_call | solution.py:539

commit v7 on v6

--- a/solution.py
+++ b/solution.py
@@ -380,7 +380,7 @@
         total = total + rows[slot, 0:1, :]
     weights = circulant_row(jnp.broadcast_to(total, (ROWS, LANES)), lons * tiles)
 
-    for copy in near_copies + cross_copies:
+    for copy in cross_copies:
         copy.wait_recv()
 
     def spread_out(x):
@@ -403,15 +403,18 @@
 
     up = jnp.where(sub > 0, 1.0, 0.0)
     down = jnp.where(sub < 1, 1.0, 0.0)
-    previous, following = [], []
-    place = 0
-    for d in beside:
+    place = len(beside) * lons
+    previous, following = [None] * place, [None] * place
+    for d in sorted(beside, key=abs):
         slot = d % tiles
+        if d:
+            near_copies[near.index(tiles - slot)].wait_recv()
         vs = spread_out(data[slot, lons * ROWS : (lons + 1) * ROWS, :])
         mixes = spread_out(jnp.broadcast_to(rows[slot, 1:2, :], (ROWS, LANES)))
         beyond = other[d + reach]
         for i in range(lons):
-            at_rows = pl.ds(place * ROWS, ROWS)
+            here = (d + reach) * lons + i
+            at_rows = pl.ds(here * ROWS, ROWS)
             f = data[slot, i * ROWS : (i + 1) * ROWS, :]
             m, u, v = mixes[i], 0.5 * to_all(f, subs - 1), 0.5 * vs[i]
             coef[0, at_rows, :] = 1.0 - 4.0 * m
@@ -419,15 +422,12 @@
             coef[2, at_rows, :] = m + u
             coef[3, at_rows, :] = jnp.where(lat == lats - 1, 0.0, m - v)
             coef[4, at_rows, :] = jnp.where(lat == 0, 0.0, m + v)
-            place += 1
             g = data[slot, (lons + 1 + i) * ROWS : (lons + 2 + i) * ROWS, :]
-            previous.append(
-                jnp.where(group == 0, up * turned(beyond, -i * span), turned(f, span))
+            previous[here] = jnp.where(
+                group == 0, up * turned(beyond, -i * span), turned(f, span)
             )
-            following.append(
-                jnp.where(
-                    group == subs - 1, down * turned(beyond, (subs - 1 - i) * span), turned(g, -span)
-                )
+            following[here] = jnp.where(
+                group == subs - 1, down * turned(beyond, (subs - 1 - i) * span), turned(g, -span)
             )
     extra = reach * lons - STEPS
     extent = place - 2 * extra

time: 14.1 us -> 13.9 us (0.986)
  Pallas kernels: 13.3 us -> 13.1 us
    pallas_call x1, Pallas kernels: 12.5 us -> 12.3 us  [direct_body(): pl.pallas_call(functools.partial(kernel, tiles, reach), out_shape=pltpu.V...]
where the time goes in v7:
time: 13.9 us; the launch traced here: 13.8 us
  Pallas kernels  13.1 us (94%)
  between operations  0.64 us (5%)
    pallas_call x1, Pallas kernels, direct_body(): pl.pallas_call(functools.partial(kernel, tiles, reach), out_shape=pltpu.V...  12.3 us
    pallas_call x1, Pallas kernels, direct_body(): pl.pallas_call(unpack, out_shape=(result, result), in_specs=[vmem], out_s...  0.82 us

profile of v7, /device:TPU:0, one launch (start us, length us, event | category | flops | bytes accessed | tf_op | source)
XLA Modules:
  0.0 13.8 jit_solution(16804660226452197051)
XLA Ops:
  0.6 12.3 %shard_map.86.packed_ref = f32[2,32,128]{2,1,0:T(8,128)S(1)} custom-call(f32[4,4,16,16]{3,2,1,0:T(8,128)} %refs_0_.1, f32[4,4,16,16]{3,2,1,0:T(8,128)} %refs_1_.1, f32[4,16,16]{2,1,0:T(8,128)} %refs_2_.1, f32[4,16,16]{2,1,0:T(8,128)} %refs_3_.1, s32[4,16]{1,0:T(4,128)} %refs_4_.1, f32[2,4]{1,0:T(2,128)} %bitcast.1, f32[4,16]{1,0:T(4,128)} %refs_6_.1), custom_call_target="tpu_custom_call" | custom-call | tf_op jit(solution)/shard_map/pallas_call | solution.py:517
  12.9 0.8 %shard_map.87 = (f32[4,4,16,16]{3,2,1,0:T(8,128)}, f32[4,4,16,16]{3,2,1,0:T(8,128)}) custom-call(f32[2,32,128]{2,1,0:T(8,128)S(1)} %shard_map.86.packed_ref), custom_call_target="tpu_custom_call" | custom-call | tf_op jit(solution)/shard_map/pallas_call | solution.py:539

commit v8 on v7

--- a/solution.py
+++ b/solution.py
@@ -346,6 +346,28 @@
         for d in range(reach, 0, -1):
             near_copy(side * d).start()
     near_copies = [near_copy(d) for d in near]
+    inc = [
+        joined([inc_ref[i, s, h * ROWS : (h + 1) * ROWS, :] for s in range(subs) for h in range(high)])
+        for i in range(lons)
+    ]
+
+    spread = jnp.zeros((ROWS, LANES), jnp.float32)
+    eye = lax.broadcasted_iota(jnp.int32, (ROWS, ROWS), 0) == lax.broadcasted_iota(
+        jnp.int32, (ROWS, ROWS), 1
+    )
+    for s in range(subs):
+        for h in range(high):
+            line = spread_ref[s : s + 1, h * ROWS : (h + 1) * ROWS]
+            column = jnp.sum(jnp.where(eye, jnp.broadcast_to(line, (ROWS, ROWS)), 0.0), 1, keepdims=True)
+            spread = jnp.where(lane // lats == s * high + h, column, spread)
+
+    for copy in row_copies:
+        copy.wait_recv()
+    total = jnp.zeros((1, LANES), jnp.float32)
+    for slot in range(tiles):
+        total = total + rows[slot, 0:1, :]
+    weights = circulant_row(jnp.broadcast_to(total, (ROWS, LANES)), lons * tiles)
+
     for d in far:
         copy = pltpu.make_async_remote_copy(
             src_ref=data.at[0, pl.ds(far_from, lons * ROWS)],
@@ -357,28 +379,6 @@
         )
         copy.start()
         far_copies.append(copy)
-
-    inc = [
-        joined([inc_ref[i, s, h * ROWS : (h + 1) * ROWS, :] for s in range(subs) for h in range(high)])
-        for i in range(lons)
-    ]
-
-    spread = jnp.zeros((ROWS, LANES), jnp.float32)
-    eye = lax.broadcasted_iota(jnp.int32, (ROWS, ROWS), 0) == lax.broadcasted_iota(
-        jnp.int32, (ROWS, ROWS), 1
-    )
-    for s in range(subs):
-        for h in range(high):
-            line = spread_ref[s : s + 1, h * ROWS : (h + 1) * ROWS]
-            column = jnp.sum(jnp.where(eye, jnp.broadcast_to(line, (ROWS, ROWS)), 0.0), 1, keepdims=True)
-            spread = jnp.where(lane // lats == s * high + h, column, spread)
-
-    for copy in row_copies:
-        copy.wait_recv()
-    total = jnp.zeros((1, LANES), jnp.float32)
-    for slot in range(tiles):
-        total = total + rows[slot, 0:1, :]
-    weights = circulant_row(jnp.broadcast_to(total, (ROWS, LANES)), lons * tiles)
 
     for copy in cross_copies:
         copy.wait_recv()

time: 13.9 us -> 15.3 us (1.10)
  Pallas kernels: 13.1 us -> 14.5 us
    pallas_call x1, Pallas kernels: 12.3 us -> 13.7 us  [direct_body(): pl.pallas_call(functools.partial(kernel, tiles, reach), out_shape=pltpu.V...]
where the time goes in v8:
time: 15.3 us; the launch traced here: 15.1 us
  Pallas kernels  14.5 us (95%)
  between operations  0.64 us (4%)
    pallas_call x1, Pallas kernels, direct_body(): pl.pallas_call(functools.partial(kernel, tiles, reach), out_shape=pltpu.V...  13.7 us
    pallas_call x1, Pallas kernels, direct_body(): pl.pallas_call(unpack, out_shape=(result, result), in_specs=[vmem], out_s...  0.82 us

profile of v8, /device:TPU:0, one launch (start us, length us, event | category | flops | bytes accessed | tf_op | source)
XLA Modules:
  0.0 15.1 jit_solution(12602360733051962591)
XLA Ops:
  0.6 13.7 %shard_map.86.packed_ref = f32[2,32,128]{2,1,0:T(8,128)S(1)} custom-call(f32[4,4,16,16]{3,2,1,0:T(8,128)} %refs_0_.1, f32[4,4,16,16]{3,2,1,0:T(8,128)} %refs_1_.1, f32[4,16,16]{2,1,0:T(8,128)} %refs_2_.1, f32[4,16,16]{2,1,0:T(8,128)} %refs_3_.1, s32[4,16]{1,0:T(4,128)} %refs_4_.1, f32[2,4]{1,0:T(2,128)} %bitcast.1, f32[4,16]{1,0:T(4,128)} %refs_6_.1), custom_call_target="tpu_custom_call" | custom-call | tf_op jit(solution)/shard_map/pallas_call | solution.py:517
  14.3 0.8 %shard_map.87 = (f32[4,4,16,16]{3,2,1,0:T(8,128)}, f32[4,4,16,16]{3,2,1,0:T(8,128)}) custom-call(f32[2,32,128]{2,1,0:T(8,128)S(1)} %shard_map.86.packed_ref), custom_call_target="tpu_custom_call" | custom-call | tf_op jit(solution)/shard_map/pallas_call | solution.py:539

commit v9 on v8

--- a/solution.py
+++ b/solution.py
@@ -329,6 +329,18 @@
         )
         copy.start()
         cross_copies.append(copy)
+    for d in far:
+        copy = pltpu.make_async_remote_copy(
+            src_ref=data.at[0, pl.ds(far_from, lons * ROWS)],
+            dst_ref=data.at[tiles - d, pl.ds(far_from, lons * ROWS)],
+            send_sem=send_sem.at[d],
+            recv_sem=recv_sem.at[tiles - d],
+            device_id={"tiles": at(d)},
+            device_id_type=MESH,
+        )
+        copy.start()
+        far_copies.append(copy)
+
     outward = jnp.where(2 * me < tiles, -1, 1)
 
     def near_copy(d):
@@ -367,18 +379,6 @@
     for slot in range(tiles):
         total = total + rows[slot, 0:1, :]
     weights = circulant_row(jnp.broadcast_to(total, (ROWS, LANES)), lons * tiles)
-
-    for d in far:
-        copy = pltpu.make_async_remote_copy(
-            src_ref=data.at[0, pl.ds(far_from, lons * ROWS)],
-            dst_ref=data.at[tiles - d, pl.ds(far_from, lons * ROWS)],
-            send_sem=send_sem.at[d],
-            recv_sem=recv_sem.at[tiles - d],
-            device_id={"tiles": at(d)},
-            device_id_type=MESH,
-        )
-        copy.start()
-        far_copies.append(copy)
 
     for copy in cross_copies:
         copy.wait_recv()

time: 15.3 us -> 14.5 us (0.948)
  Pallas kernels: 14.5 us -> 13.7 us
    pallas_call x1, Pallas kernels: 13.7 us -> 12.9 us  [direct_body(): pl.pallas_call(functools.partial(kernel, tiles, reach), out_shape=pltpu.V...]
where the time goes in v9:
time: 14.5 us; the launch traced here: 14.4 us
  Pallas kernels  13.7 us (94%)
  between operations  0.64 us (4%)
    pallas_call x1, Pallas kernels, direct_body(): pl.pallas_call(functools.partial(kernel, tiles, reach), out_shape=pltpu.V...  12.9 us
    pallas_call x1, Pallas kernels, direct_body(): pl.pallas_call(unpack, out_shape=(result, result), in_specs=[vmem], out_s...  0.82 us

profile of v9, /device:TPU:0, one launch (start us, length us, event | category | flops | bytes accessed | tf_op | source)
XLA Modules:
  0.0 14.4 jit_solution(17116330940126571691)
XLA Ops:
  0.6 12.9 %shard_map.86.packed_ref = f32[2,32,128]{2,1,0:T(8,128)S(1)} custom-call(f32[4,4,16,16]{3,2,1,0:T(8,128)} %refs_0_.1, f32[4,4,16,16]{3,2,1,0:T(8,128)} %refs_1_.1, f32[4,16,16]{2,1,0:T(8,128)} %refs_2_.1, f32[4,16,16]{2,1,0:T(8,128)} %refs_3_.1, s32[4,16]{1,0:T(4,128)} %refs_4_.1, f32[2,4]{1,0:T(2,128)} %bitcast.1, f32[4,16]{1,0:T(4,128)} %refs_6_.1), custom_call_target="tpu_custom_call" | custom-call | tf_op jit(solution)/shard_map/pallas_call | solution.py:517
  13.6 0.8 %shard_map.87 = (f32[4,4,16,16]{3,2,1,0:T(8,128)}, f32[4,4,16,16]{3,2,1,0:T(8,128)}) custom-call(f32[2,32,128]{2,1,0:T(8,128)S(1)} %shard_map.86.packed_ref), custom_call_target="tpu_custom_call" | custom-call | tf_op jit(solution)/shard_map/pallas_call | solution.py:539
